TPU v7x, 32 devices: a whole 2x2x4 slice. The times are simulated.
32 devices in a mesh: tx: 4 (over y, x), ty: 8 (over z, core).
Axes of the slice: x: 2, y: 2, z: 4, core: 2. Of those that a mesh axis runs over, the one named last changes fastest.
Arguments:
- pressure: float32 [80, 64, 2048], P(None, 'tx', 'ty'), may hold values from -6 to 6
- velocity: float32 [3, 80, 64, 2048], P(None, None, 'tx', 'ty'), may hold values from -6 to 6
- kappa: float32 [80, 64, 2048], P(None, 'tx', 'ty'), may hold values from 0.05 to 0.5
- buoyancy: float32 [3, 80, 64, 2048], P(None, None, 'tx', 'ty'), may hold values from 0.1 to 1
- fwd_pressure: float32 [2, 80, 64, 2048], P(None, None, 'tx', 'ty'), may hold values from -6 to 6
- gradient: float32 [80, 64, 2048], P(None, 'tx', 'ty'), may hold values from -6 to 6
- traces: float32 [32768, 256], P(('tx', 'ty')), may hold values from -6 to 6
- kernel: float32 [2, 256], replicated, may hold values from -0.75 to 0.75
- rec_tile: int32 [32768, 1], P(('tx', 'ty')), may hold values from 0 to 31; in each aligned block of 1024 rows (0 to 1023, 1024 to 2047, ...) at most 64 rows name the same one
- rec_cell: int32 [32768], P(('tx', 'ty')), may hold values from 0 to 4095
Outputs:
- pressure_out: float32 [80, 64, 2048], P(None, 'tx', 'ty')
- velocity_out: float32 [3, 80, 64, 2048], P(None, None, 'tx', 'ty')
- gradient_out: float32 [80, 64, 2048], P(None, 'tx', 'ty')
Inputs may be any that keep to these rules, and one draw needn't show every extreme that they name: `rec_tile`: in each aligned block of 1024 rows (the rows of one device) no tile is named by more than 64 rows, a bound that some block reaches.
All inputs are finite; a program needn't handle non-finite values.
Results may differ from a plain program's by a relative error of at most 0.00009.
Values sent between devices are 32-bit elements; how exact they have to be, the bound alone decides.
A program may use at most 128 MiB of HBM per device.

v0:
```python
import jax
import jax.numpy as jnp
from jax import lax
from jax.sharding import PartitionSpec as P

STEPS = 2
REC_DEPTH = 3


coeffs = (1225.0 / 1024.0, -245.0 / 3072.0, 49.0 / 5120.0, -5.0 / 7168.0)


def extended(value, sides, width):
    for axis, dim in sides:
        devices, length = (lax.axis_size(axis), value.shape[dim])
        up = [(i, (i + 1) % devices) for i in range(devices - 1)]
        down = [(j, i) for i, j in up]
        last = lax.slice_in_dim(value, length - width, length, axis=dim)
        initial = lax.slice_in_dim(value, 0, width, axis=dim)
        before = lax.ppermute(last, axis, up)
        after = lax.ppermute(initial, axis, down)
        value = jnp.concatenate([before, value, after], axis=dim)
    return value


def along(field, axis, start, count):
    return lax.slice_in_dim(field, start, start + count, axis=axis)


def plus_diff(field, axis, count):
    total = coeffs[0] * (along(field, axis, 5, count) - along(field, axis, 4, count))
    for k in range(2, 5):
        total = total + coeffs[k - 1] * (
            along(field, axis, 4 + k, count) - along(field, axis, 5 - k, count)
        )
    return total


def minus_diff(field, axis, count):
    total = coeffs[0] * (along(field, axis, 4, count) - along(field, axis, 3, count))
    for k in range(2, 5):
        total = total + coeffs[k - 1] * (
            along(field, axis, 3 + k, count) - along(field, axis, 4 - k, count)
        )
    return total


def local(
    pressure, velocity, kappa, buoyancy, fwd_pressure, gradient, traces, kernel, rec_tile, rec_cell
):
    nz, cx, cy = pressure.shape
    rows, samples = traces.shape
    steps = kernel.shape[0]
    devices = lax.axis_size(("tx", "ty"))
    slots = max(4, 2 * rows // devices)
    plane_cells = cx * cy
    tiles = rec_tile[:, 0]
    onehot = (tiles[:, None] == jnp.arange(devices, dtype=jnp.int32)[None, :]).astype(jnp.int32)
    rank = jnp.sum((jnp.cumsum(onehot, axis=0) - 1) * onehot, axis=1)
    slot = tiles * slots + rank
    empty_cells = jnp.full((devices * slots,), plane_cells, jnp.int32).at[slot].set(rec_cell)
    filtered = jnp.einsum("sk,rk->sr", kernel, traces, precision=lax.Precision.HIGHEST)
    sample_buf = jnp.zeros((steps, devices * slots), jnp.float32).at[:, slot].set(filtered)
    sources, cell_rows = (
        lax.all_to_all(sample_buf, ("tx", "ty"), split_axis=1, concat_axis=1, tiled=True),
        lax.all_to_all(empty_cells[None, :], ("tx", "ty"), split_axis=1, concat_axis=1, tiled=True),
    )
    cells = cell_rows[0]
    inject = jnp.zeros((steps, plane_cells + 1), jnp.float32).at[:, cells].add(sources)
    inject = inject[:, :plane_cells].reshape(steps, cx, cy)
    press = pressure
    vel_x, vel_y, vel_z = (velocity[0], velocity[1], velocity[2])
    grad = gradient
    for step in range(STEPS):
        padded = extended(press, (("tx", 1), ("ty", 2)), 4)
        vel_x = vel_x - buoyancy[0] * plus_diff(padded[:, :, 4 : 4 + cy], 1, cx)
        vel_y = vel_y - buoyancy[1] * plus_diff(padded[:, 4 : 4 + cx, :], 2, cy)
        zpadded = jnp.pad(press, ((4, 4), (0, 0), (0, 0)))
        vel_z = vel_z - buoyancy[2] * plus_diff(zpadded, 0, nz)
        xpad = extended(vel_x, (("tx", 1),), 4)
        ypad = extended(vel_y, (("ty", 2),), 4)
        zpad = jnp.pad(vel_z, ((4, 4), (0, 0), (0, 0)))
        diverge = minus_diff(xpad, 1, cx) + minus_diff(ypad, 2, cy) + minus_diff(zpad, 0, nz)
        press = press - kappa * diverge
        press = press.at[REC_DEPTH].add(inject[step])
        grad = grad + fwd_pressure[step] * press
    return (press, jnp.stack([vel_x, vel_y, vel_z]), grad)


def solution(mesh):
    return jax.shard_map(
        local,
        mesh=mesh,
        in_specs=(
            P(None, "tx", "ty"),
            P(None, None, "tx", "ty"),
            P(None, "tx", "ty"),
            P(None, None, "tx", "ty"),
            P(None, None, "tx", "ty"),
            P(None, "tx", "ty"),
            P(("tx", "ty"), None),
            P(),
            P(("tx", "ty"), None),
            P(("tx", "ty")),
        ),
        out_specs=(P(None, "tx", "ty"), P(None, None, "tx", "ty"), P(None, "tx", "ty")),
        check_vma=False,
    )
```

profile of v0, /device:TPU:0, one launch (start us, length us, event | category | flops | bytes accessed | tf_op | source)
XLA Modules:
  0.0 214.0 jit_solution(9351301011230358125)
XLA Ops:
  0.7 2.3 %fusion.190 = (f32[80,4,256]{2,1,0:T(4,128)}, f32[80,4,256]{2,1,0:T(4,128)}) fusion(f32[80,16,256]{2,1,0:T(8,128)} %param.14), kind=kLoop, calls=%fused_computation.316 | loop fusion | bytes 1310720 | tf_op jit(solution)/shard_map/slice | solution.py:18
  3.0 1.3 collective-permute-start
  4.3 5.5 %collective-permute-start.1 = (f32[80,4,256]{2,1,0:T(4,128)}, f32[80,4,256]{2,1,0:T(4,128)S(1)}, u32[]{:S(2)}, u32[]{:S(2)}) collective-permute-start(f32[80,4,256]{2,1,0:T(4,128)} %get-tuple-element.53), channel_id=1, source_target_pairs={{0,8},{8,16},{16,24},{1,9},{9,17},{17,25},{2,10},{10,18},{18,26},{... | collective-permute-start | bytes 983048 | tf_op jit(solution)/shard_map/ppermute | solution.py:20
  9.8 9.0 %reduce-window.6 = s32[32,8,128]{2,1,0:T(8,128)S(1)} reduce-window(s32[32,8,128]{2,1,0:T(8,128)S(1)} %fusion.178, s32[]{:T(128)} %constant.74.clone.1), window={size=1x1x128 pad=0_0x0_0x127_0}, to_apply=%region_0.0 | reduce-window | flops 4161536 | bytes 262148 | tf_op jit(solution)/shard_map/reduce-window
  19.3 4.5 %scatter_custom_fusion = s32[2048]{0:T(1024)S(1)} fusion(s32[1024]{0:T(1024)S(1)} %bitcast.67, s32[1024]{0:T(1024)} %param.23, s32[]{:T(128)} %constant.72.clone.1), kind=kCustom, calls=%fused_computation.307 | custom fusion | bytes 8704 | tf_op jit(solution)/shard_map/scatter | solution.py:61
  23.8 0.7 all_to_all.14
  24.5 6.3 %all-to-all-start = ((s32[1,32,64]{2,0,1:T(1,128)}), s32[1,32,64]{2,0,1:T(1,128)S(1)}, u32[]{:S(2)}, u32[]{:S(2)}) async-start(s32[1,32,64]{2,0,1:T(1,128)} %all_to_all.14), calls=%async_computation | async-start | bytes 32768 | tf_op jit(solution)/shard_map/all_to_all | solution.py:66
  30.9 0.9 fusion.191
  31.8 3.6 %scatter_custom_fusion.1 = f32[2,2048]{0,1:T(8,128)S(1)} fusion(s32[1024]{0:T(1024)} %bitcast.68, f32[1024,2]{1,0:T(8,128)S(1)} %fusion.191, f32[]{:T(128)} %constant.71.clone.1), kind=kCustom, calls=%fused_computation.290 | custom fusion | bytes 16896 | tf_op jit(solution)/shard_map/scatter | solution.py:63
  35.4 0.4 copy.48
  35.8 0.7 reshape.169
  36.5 1.4 all-to-all-done
  37.9 4.5 %all-to-all-start.1 = ((f32[32,1,128]{2,1,0:T(1,128)}), f32[32,1,128]{2,1,0:T(1,128)S(1)}, u32[]{:S(2)}, u32[]{:S(2)}) async-start(f32[32,1,128]{2,1,0:T(1,128)} %reshape.169), calls=%async_computation.1 | async-start | bytes 32768 | tf_op jit(solution)/shard_map/all_to_all | solution.py:65
  42.4 0.5 broadcast.141
  42.9 0.7 reduce.11
  43.7 0.7 copy-done.11
  44.4 0.7 copy-done.13
  46.1 1.3 collective-permute-start.4
  47.7 3.0 %collective-permute-start.5 = (f32[80,24,4]{0,1,2:T(8,128)S(1)}, f32[80,24,4]{0,1,2:T(8,128)S(1)}, u32[]{:S(2)}, u32[]{:S(2)}) collective-permute-start(f32[80,24,4]{0,1,2:T(8,128)S(1)} %copy.39), channel_id=1, source_target_pairs={{0,1},{1,2},{2,3},{3,4},{4,5},{5,6},{6,7},{8,9},{9,10},{10,11},{11... | collective-permute-start | bytes 92168 | tf_op jit(solution)/shard_map/ppermute | solution.py:20
  50.8 0.5 broadcast.142
  51.3 0.7 reduce.12
  52.6 13.7 %scatter_custom_fusion.2 = f32[2,4097]{0,1:T(8,128)} fusion(s32[2048]{0:T(1024)S(1)} %bitcast.66, f32[2048,2]{1,0:T(8,128)S(1)} %copy.50, f32[]{:T(128)} %constant.71.clone.1), kind=kCustom, calls=%fused_computation.288 | custom fusion | flops 4096 | bytes 32780 | tf_op jit(solution)/shard_map/scatter-add | solution.py:69
  66.2 0.4 copy.38
  66.7 0.4 copy.40
  67.1 4.9 %pad_maximum_fusion.1 = (f32[80,24,260]{2,1,0:T(8,128)}, f32[80,24,260]{2,1,0:T(8,128)}) fusion(f32[80,24,4]{2,1,0:T(8,128)S(1)} %copy.38, f32[80,4,256]{2,1,0:T(4,128)} %copy-done.11, f32[80,16,256]{2,1,0:T(8,128)S(1)} %copy-done.2, f32[80,4,256]{2,1,0:T(4,128)} %copy-done.13, f32[80,24,4]{2,1,0:T(8,128)S(1)} %copy.40), kind=kLoop, calls=%fused_computation.19 | loop fusion | flops 2995200 | bytes 6021120 | tf_op jit(solution)/shard_map/concatenate | solution.py:22
  72.0 11.8 %constant_dynamic-update-slice_fusion.1 = (f32[80,20,256]{2,1,0:T(8,128)}, f32[80,16,256]{2,1,0:T(8,128)}) fusion(f32[80,16,256]{2,1,0:T(8,128)S(1)} %copy-done.2, f32[80,24,260]{2,1,0:T(8,128)} %get-tuple-element.38, f32[80,24,260]{2,1,0:T(8,128)} %get-tuple-element.37, f32[3,80,16,256]{3,2,1,0:T(8,128)} %param.17, f32[3,80,16,256]{3,2,1,0:T(8,128)} %param.15), kind=kLoop, calls=%fused_computation.306 | loop fusion | flops 4259839 | bytes 15728640
  83.8 0.8 constant_dynamic-update-slice_fusion
  84.6 7.6 %fusion.109 = (f32[80,16,256]{2,1,0:T(8,128)S(1)}, f32[80,16,256]{2,1,0:T(8,128)}) fusion(f32[80,16,256]{2,1,0:T(8,128)S(1)} %copy-done.2, f32[80,4,256]{2,1,0:T(4,128)S(1)} %copy-done.14, f32[80,20,256]{2,1,0:T(8,128)} %constant_dynamic-update-slice_fusion, f32[3,80,16,256]{3,2,1,0:T(8,128)} %param.15, f32[3,80,16,256]{3,2,1,0:T(8,128)} %param.17), kind=kLoop, calls=%fused_computation.203 | loop fusion | flops 9502720 | bytes 14745600 | tf_op jit(solution)/shard_map/sub | solution.py:76
  92.2 0.9 fusion.188
  93.2 4.8 %collective-permute-start.2 = (f32[80,4,256]{2,1,0:T(4,128)}, f32[80,4,256]{2,1,0:T(4,128)S(1)}, u32[]{:S(2)}, u32[]{:S(2)}) collective-permute-start(f32[80,4,256]{2,1,0:T(4,128)} %get-tuple-element.47), channel_id=1, source_target_pairs={{0,8},{8,16},{16,24},{1,9},{9,17},{17,25},{2,10},{10,18},{18,26},{... | collective-permute-start | bytes 983048 | tf_op jit(solution)/shard_map/ppermute | solution.py:20
  97.9 1.3 collective-permute-start.3
  99.2 1.1 fusion.189
  100.3 1.4 copy.41
  101.7 2.8 %collective-permute-start.6 = (f32[80,16,4]{0,1,2:T(8,128)S(1)}, f32[80,16,4]{0,1,2:T(8,128)S(1)}, u32[]{:S(2)}, u32[]{:S(2)}) collective-permute-start(f32[80,16,4]{0,1,2:T(8,128)S(1)} %copy.41), channel_id=1, source_target_pairs={{0,1},{1,2},{2,3},{3,4},{4,5},{5,6},{6,7},{8,9},{9,10},{10,11},{11... | collective-permute-start | bytes 61448 | tf_op jit(solution)/shard_map/ppermute | solution.py:20
  104.5 0.9 copy.43
  105.4 1.3 collective-permute-start.7
  106.7 1.7 slice_reduce_fusion
  108.5 0.4 copy.42
  108.8 1.1 copy.44
  110.0 4.2 %collective-permute-done.3 = f32[80,4,256]{2,1,0:T(4,128)S(1)} collective-permute-done((f32[80,4,256]{2,1,0:T(4,128)}, f32[80,4,256]{2,1,0:T(4,128)S(1)}, u32[]{:S(2)}, u32[]{:S(2)}) %collective-permute-start.3) | collective-permute-done | bytes 327712 | tf_op jit(solution)/shard_map/ppermute | solution.py:21
  114.2 16.2 %fusion.20 = f32[80,16,256]{2,1,0:T(8,128)S(1)} fusion(f32[80,16,256]{2,1,0:T(8,128)} %param.14, f32[80,16,256]{2,1,0:T(8,128)} %param.16, f32[80,16,256]{2,1,0:T(8,128)} %get-tuple-element.30, f32[80,16,256]{2,1,0:T(8,128)} %get-tuple-element.52, f32[80,16,256]{2,1,0:T(8,128)} %copy-done.6, f32[80,16,4]{2,1,0:T(8,128)S(1)} %copy.44, ...), kind=kLoop, calls=%fused_computation.114 | loop fusion | flops 16711680 | bytes 8560640 | tf_op jit(solution)/shard_map/sub | solution.py:84
  130.5 1.3 collective-permute-start.8
  131.8 4.8 %collective-permute-start.9 = (f32[80,4,256]{2,1,0:T(4,128)S(1)}, f32[80,4,256]{2,1,0:T(4,128)S(1)}, u32[]{:S(2)}, u32[]{:S(2)}) collective-permute-start(f32[80,4,256]{2,1,0:T(4,128)S(1)} %get-tuple-element.45), channel_id=1, source_target_pairs={{0,8},{8,16},{16,24},{1,9},{9,17},{17,25},{2,10},{10,18},{18,26},{... | collective-permute-start | bytes 983048 | tf_op jit(solution)/shard_map/ppermute | solution.py:20
  136.6 6.3 %collective-permute-done.8 = f32[80,4,256]{2,1,0:T(4,128)S(1)} collective-permute-done((f32[80,4,256]{2,1,0:T(4,128)S(1)}, f32[80,4,256]{2,1,0:T(4,128)S(1)}, u32[]{:S(2)}, u32[]{:S(2)}) %collective-permute-start.8) | collective-permute-done | bytes 327712 | tf_op jit(solution)/shard_map/ppermute | solution.py:21
  142.9 0.7 collective-permute-done.9
  143.7 0.7 copy-done.10
  145.4 1.3 collective-permute-start.12
  147.0 3.0 %collective-permute-start.13 = (f32[80,24,4]{0,1,2:T(8,128)S(1)}, f32[80,24,4]{0,1,2:T(8,128)S(1)}, u32[]{:S(2)}, u32[]{:S(2)}) collective-permute-start(f32[80,24,4]{0,1,2:T(8,128)S(1)} %copy.53), channel_id=1, source_target_pairs={{0,1},{1,2},{2,3},{3,4},{4,5},{5,6},{6,7},{8,9},{9,10},{10,11},{11... | collective-permute-start | bytes 92168 | tf_op jit(solution)/shard_map/ppermute | solution.py:20
  150.1 5.7 %fusion.79 = (f32[80,16,256]{2,1,0:T(8,128)S(1)}, f32[80,16,256]{2,1,0:T(8,128)}) fusion(f32[80,16,256]{2,1,0:T(8,128)} %copy-done.6, f32[80,16,256]{2,1,0:T(8,128)S(1)} %fusion.180, f32[80,4,256]{2,1,0:T(4,128)} %copy-done.10, f32[80,4,256]{2,1,0:T(4,128)} %copy-done.9, f32[3,80,16,256]{3,2,1,0:T(8,128)} %param.17, f32[80,16,256]{2,1,0:T(8,128)} %get-tuple-element.30), kind=kLoop, calls=%fused_computation.173 | loop fusion | flops 10813440 | bytes 9830400 | tf_op jit(solution)/shard_map/sub | solution.py:76
  155.8 1.1 copy-done.7
  156.9 0.9 fusion.185
  157.8 8.0 %collective-permute-start.10 = (f32[80,4,256]{2,1,0:T(4,128)}, f32[80,4,256]{2,1,0:T(4,128)}, u32[]{:S(2)}, u32[]{:S(2)}) collective-permute-start(f32[80,4,256]{2,1,0:T(4,128)} %get-tuple-element.41), channel_id=1, source_target_pairs={{0,8},{8,16},{16,24},{1,9},{9,17},{17,25},{2,10},{10,18},{18,26},{... | collective-permute-start | bytes 983048 | tf_op jit(solution)/shard_map/ppermute | solution.py:20
  165.8 1.3 collective-permute-start.11
  167.1 0.4 copy.52
  167.5 0.4 copy.54
  167.9 4.8 %pad_maximum_fusion.2 = (f32[80,24,260]{2,1,0:T(8,128)}, f32[80,24,260]{2,1,0:T(8,128)}) fusion(f32[80,24,4]{2,1,0:T(8,128)S(1)} %copy.52, f32[80,4,256]{2,1,0:T(4,128)} %copy-done.9, f32[80,16,256]{2,1,0:T(8,128)S(1)} %fusion.180, f32[80,4,256]{2,1,0:T(4,128)} %copy-done.10, f32[80,24,4]{2,1,0:T(8,128)S(1)} %copy.54), kind=kLoop, calls=%fused_computation.21 | loop fusion | flops 2995200 | bytes 6021120 | tf_op jit(solution)/shard_map/concatenate | solution.py:22
  172.8 11.1 %fusion.144 = f32[80,16,256]{2,1,0:T(8,128)} fusion(f32[80,16,256]{2,1,0:T(8,128)S(1)} %copy-done.4, f32[80,24,260]{2,1,0:T(8,128)} %get-tuple-element.34, f32[80,24,260]{2,1,0:T(8,128)} %get-tuple-element.33, f32[80,16,256]{2,1,0:T(8,128)S(1)} %fusion.180, f32[3,80,16,256]{3,2,1,0:T(8,128)} %param.17), kind=kLoop, calls=%fused_computation.241 | loop fusion | flops 4259840 | bytes 14417920 | tf_op jit(solution)/shard_map/sub | solution.py:77
  183.9 1.5 fusion.186
  185.7 2.6 %collective-permute-start.14 = (f32[80,16,4]{0,1,2:T(8,128)S(1)}, f32[80,16,4]{0,1,2:T(8,128)S(1)}, u32[]{:S(2)}, u32[]{:S(2)}) collective-permute-start(f32[80,16,4]{0,1,2:T(8,128)S(1)} %copy.55), channel_id=1, source_target_pairs={{0,1},{1,2},{2,3},{3,4},{4,5},{5,6},{6,7},{8,9},{9,10},{10,11},{11... | collective-permute-start | bytes 61448 | tf_op jit(solution)/shard_map/ppermute | solution.py:20
  188.6 1.5 collective-permute-start.15
  190.2 4.4 %pad_maximum_fusion = f32[3,80,16,256]{3,2,1,0:T(8,128)} fusion(f32[1,80,16,256]{3,2,1,0:T(8,128)} %bitcast.56, f32[1,80,16,256]{3,2,1,0:T(8,128)} %bitcast.54, f32[1,80,16,256]{3,2,1,0:T(8,128)} %bitcast.55), kind=kLoop, calls=%fused_computation.3 | loop fusion | flops 1966080 | bytes 7864320 | tf_op jit(solution)/shard_map/stack | solution.py:87
  195.0 0.4 copy.58
  195.4 16.6 %fusion.47 = f32[80,16,256]{2,1,0:T(8,128)S(1)} fusion(f32[80,16,256]{2,1,0:T(8,128)S(1)} %fusion.180, f32[80,16,256]{2,1,0:T(8,128)} %param.16, f32[80,16,256]{2,1,0:T(8,128)} %get-tuple-element.32, f32[80,16,256]{2,1,0:T(8,128)} %fusion.144, f32[80,16,256]{2,1,0:T(8,128)} %copy-done.7, f32[80,16,4]{2,1,0:T(8,128)S(1)} %copy.58, ...), kind=kLoop, calls=%fused_computation.141 | loop fusion | flops 16711680 | bytes 8560640 | tf_op jit(solution)/shard_map/sub | solution.py:84
  212.1 1.9 fusion.170
  (81 shorter events, 5.2 us)
Async XLA Ops:
  0.6 30.2 %copy-start = (f32[1024,256]{1,0:T(8,128)S(1)}, f32[1024,256]{1,0:T(8,128)}, u32[]{:S(2)}) copy-start(f32[1024,256]{1,0:T(8,128)} %param.20) | copy-start | bytes 3145732
  0.6 9.1 %copy-start.17 = (s32[1024,1]{0,1:T(1,128)S(1)}, s32[1024,1]{0,1:T(1,128)}, u32[]{:S(2)}) copy-start(s32[1024,1]{0,1:T(1,128)} %param.22) | copy-start | bytes 12292
  0.7 30.2 %copy-start.19 = (f32[2,256]{1,0:T(2,128)S(1)}, f32[2,256]{1,0:T(2,128)}, u32[]{:S(2)}) copy-start(f32[2,256]{1,0:T(2,128)} %param.21) | copy-start | bytes 6148
  3.0 40.7 %collective-permute-start = (f32[80,4,256]{2,1,0:T(4,128)}, f32[80,4,256]{2,1,0:T(4,128)S(1)}, u32[]{:S(2)}, u32[]{:S(2)}) collective-permute-start(f32[80,4,256]{2,1,0:T(4,128)} %get-tuple-element.54), channel_id=1, source_target_pairs={{8,0},{16,8},{24,16},{9,1},{17,9},{25,17},{10,2},{18,10},{26,18},{... | collective-permute-start | bytes 983048 | tf_op jit(solution)/shard_map/ppermute | solution.py:21
  4.3 39.4 %collective-permute-start.1 = (f32[80,4,256]{2,1,0:T(4,128)}, f32[80,4,256]{2,1,0:T(4,128)S(1)}, u32[]{:S(2)}, u32[]{:S(2)}) collective-permute-start(f32[80,4,256]{2,1,0:T(4,128)} %get-tuple-element.53), channel_id=1, source_target_pairs={{0,8},{8,16},{16,24},{1,9},{9,17},{17,25},{2,10},{10,18},{18,26},{... | collective-permute-start | bytes 983048 | tf_op jit(solution)/shard_map/ppermute | solution.py:20
  19.3 11.5 %copy-start.18 = (s32[1024,1]{0,1:T(1,128)}, s32[1024,1]{0,1:T(1,128)S(1)}, u32[]{:S(2)}) copy-start(s32[1024,1]{0,1:T(1,128)S(1)} %compare_select_fusion.1) | copy-start | bytes 12292
  24.5 13.4 %all-to-all-start = ((s32[1,32,64]{2,0,1:T(1,128)}), s32[1,32,64]{2,0,1:T(1,128)S(1)}, u32[]{:S(2)}, u32[]{:S(2)}) async-start(s32[1,32,64]{2,0,1:T(1,128)} %all_to_all.14), calls=%async_computation | async-start | bytes 32768 | tf_op jit(solution)/shard_map/all_to_all | solution.py:66
  31.8 13.3 %copy-start.2 = (f32[80,16,256]{2,1,0:T(8,128)S(1)}, f32[80,16,256]{2,1,0:T(8,128)}, u32[]{:S(2)}) copy-start(f32[80,16,256]{2,1,0:T(8,128)} %param.14) | copy-start | bytes 3932164
  37.9 12.9 %all-to-all-start.1 = ((f32[32,1,128]{2,1,0:T(1,128)}), f32[32,1,128]{2,1,0:T(1,128)S(1)}, u32[]{:S(2)}, u32[]{:S(2)}) async-start(f32[32,1,128]{2,1,0:T(1,128)} %reshape.169), calls=%async_computation.1 | async-start | bytes 32768 | tf_op jit(solution)/shard_map/all_to_all | solution.py:65
  43.7 0.7 copy-start.11
  44.4 0.7 copy-start.13
  46.1 20.2 %collective-permute-start.4 = (f32[80,24,4]{0,1,2:T(8,128)S(1)}, f32[80,24,4]{0,1,2:T(8,128)S(1)}, u32[]{:S(2)}, u32[]{:S(2)}) collective-permute-start(f32[80,24,4]{0,1,2:T(8,128)S(1)} %copy.37), channel_id=1, source_target_pairs={{1,0},{2,1},{3,2},{4,3},{5,4},{6,5},{7,6},{9,8},{10,9},{11,10},{12... | collective-permute-start | bytes 92168 | tf_op jit(solution)/shard_map/ppermute | solution.py:21
  47.7 18.9 %collective-permute-start.5 = (f32[80,24,4]{0,1,2:T(8,128)S(1)}, f32[80,24,4]{0,1,2:T(8,128)S(1)}, u32[]{:S(2)}, u32[]{:S(2)}) collective-permute-start(f32[80,24,4]{0,1,2:T(8,128)S(1)} %copy.39), channel_id=1, source_target_pairs={{0,1},{1,2},{2,3},{3,4},{4,5},{5,6},{6,7},{8,9},{9,10},{10,11},{11... | collective-permute-start | bytes 92168 | tf_op jit(solution)/shard_map/ppermute | solution.py:20
  72.0 11.8 %copy-start.12 = (f32[80,4,256]{2,1,0:T(4,128)S(1)}, f32[80,4,256]{2,1,0:T(4,128)}, u32[]{:S(2)}) copy-start(f32[80,4,256]{2,1,0:T(4,128)} %copy-done.11) | copy-start | bytes 983044
  72.0 12.6 %copy-start.14 = (f32[80,4,256]{2,1,0:T(4,128)S(1)}, f32[80,4,256]{2,1,0:T(4,128)}, u32[]{:S(2)}) copy-start(f32[80,4,256]{2,1,0:T(4,128)} %copy-done.13) | copy-start | bytes 983044
  92.2 8.1 %copy-start.6 = (f32[80,16,256]{2,1,0:T(8,128)}, f32[80,16,256]{2,1,0:T(8,128)S(1)}, u32[]{:S(2)}) copy-start(f32[80,16,256]{2,1,0:T(8,128)S(1)} %get-tuple-element.29) | copy-start | bytes 3932164
  92.2 7.0 %copy-start.3 = (f32[80,16,256]{2,1,0:T(8,128)S(1)}, f32[80,16,256]{2,1,0:T(8,128)}, u32[]{:S(2)}) copy-start(f32[80,16,256]{2,1,0:T(8,128)} %get-tuple-element.52) | copy-start | bytes 3932164
  93.2 16.8 %collective-permute-start.2 = (f32[80,4,256]{2,1,0:T(4,128)}, f32[80,4,256]{2,1,0:T(4,128)S(1)}, u32[]{:S(2)}, u32[]{:S(2)}) collective-permute-start(f32[80,4,256]{2,1,0:T(4,128)} %get-tuple-element.47), channel_id=1, source_target_pairs={{0,8},{8,16},{16,24},{1,9},{9,17},{17,25},{2,10},{10,18},{18,26},{... | collective-permute-start | bytes 983048 | tf_op jit(solution)/shard_map/ppermute | solution.py:20
  97.9 16.2 %collective-permute-start.3 = (f32[80,4,256]{2,1,0:T(4,128)}, f32[80,4,256]{2,1,0:T(4,128)S(1)}, u32[]{:S(2)}, u32[]{:S(2)}) collective-permute-start(f32[80,4,256]{2,1,0:T(4,128)} %get-tuple-element.48), channel_id=1, source_target_pairs={{8,0},{16,8},{24,16},{9,1},{17,9},{25,17},{10,2},{18,10},{26,18},{... | collective-permute-start | bytes 983048 | tf_op jit(solution)/shard_map/ppermute | solution.py:21
  99.2 7.5 %copy-start.5 = (f32[2,4097]{0,1:T(8,128)S(1)}, f32[2,4097]{0,1:T(8,128)}, u32[]{:S(2)}) copy-start(f32[2,4097]{0,1:T(8,128)} %scatter_custom_fusion.2) | copy-start | bytes 98332
  101.7 6.7 %collective-permute-start.6 = (f32[80,16,4]{0,1,2:T(8,128)S(1)}, f32[80,16,4]{0,1,2:T(8,128)S(1)}, u32[]{:S(2)}, u32[]{:S(2)}) collective-permute-start(f32[80,16,4]{0,1,2:T(8,128)S(1)} %copy.41), channel_id=1, source_target_pairs={{0,1},{1,2},{2,3},{3,4},{4,5},{5,6},{6,7},{8,9},{9,10},{10,11},{11... | collective-permute-start | bytes 61448 | tf_op jit(solution)/shard_map/ppermute | solution.py:20
  105.4 3.4 %collective-permute-start.7 = (f32[80,16,4]{0,1,2:T(8,128)}, f32[80,16,4]{0,1,2:T(8,128)}, u32[]{:S(2)}, u32[]{:S(2)}) collective-permute-start(f32[80,16,4]{0,1,2:T(8,128)} %copy.43), channel_id=1, source_target_pairs={{1,0},{2,1},{3,2},{4,3},{5,4},{6,5},{7,6},{9,8},{10,9},{11,10},{12... | collective-permute-start | bytes 61448 | tf_op jit(solution)/shard_map/ppermute | solution.py:21
  130.5 12.4 %collective-permute-start.8 = (f32[80,4,256]{2,1,0:T(4,128)S(1)}, f32[80,4,256]{2,1,0:T(4,128)S(1)}, u32[]{:S(2)}, u32[]{:S(2)}) collective-permute-start(f32[80,4,256]{2,1,0:T(4,128)S(1)} %get-tuple-element.46), channel_id=1, source_target_pairs={{8,0},{16,8},{24,16},{9,1},{17,9},{25,17},{10,2},{18,10},{26,18},{... | collective-permute-start | bytes 983048 | tf_op jit(solution)/shard_map/ppermute | solution.py:21
  131.8 11.8 %collective-permute-start.9 = (f32[80,4,256]{2,1,0:T(4,128)S(1)}, f32[80,4,256]{2,1,0:T(4,128)S(1)}, u32[]{:S(2)}, u32[]{:S(2)}) collective-permute-start(f32[80,4,256]{2,1,0:T(4,128)S(1)} %get-tuple-element.45), channel_id=1, source_target_pairs={{0,8},{8,16},{16,24},{1,9},{9,17},{17,25},{2,10},{10,18},{18,26},{... | collective-permute-start | bytes 983048 | tf_op jit(solution)/shard_map/ppermute | solution.py:20
  142.9 0.7 copy-start.9
  143.7 0.7 copy-start.10
  145.4 21.7 %collective-permute-start.12 = (f32[80,24,4]{0,1,2:T(8,128)S(1)}, f32[80,24,4]{0,1,2:T(8,128)S(1)}, u32[]{:S(2)}, u32[]{:S(2)}) collective-permute-start(f32[80,24,4]{0,1,2:T(8,128)S(1)} %copy.51), channel_id=1, source_target_pairs={{1,0},{2,1},{3,2},{4,3},{5,4},{6,5},{7,6},{9,8},{10,9},{11,10},{12... | collective-permute-start | bytes 92168 | tf_op jit(solution)/shard_map/ppermute | solution.py:21
  147.0 20.4 %collective-permute-start.13 = (f32[80,24,4]{0,1,2:T(8,128)S(1)}, f32[80,24,4]{0,1,2:T(8,128)S(1)}, u32[]{:S(2)}, u32[]{:S(2)}) collective-permute-start(f32[80,24,4]{0,1,2:T(8,128)S(1)} %copy.53), channel_id=1, source_target_pairs={{0,1},{1,2},{2,3},{3,4},{4,5},{5,6},{6,7},{8,9},{9,10},{10,11},{11... | collective-permute-start | bytes 92168 | tf_op jit(solution)/shard_map/ppermute | solution.py:20
  155.8 1.1 copy-start.7
  157.8 37.6 %collective-permute-start.10 = (f32[80,4,256]{2,1,0:T(4,128)}, f32[80,4,256]{2,1,0:T(4,128)}, u32[]{:S(2)}, u32[]{:S(2)}) collective-permute-start(f32[80,4,256]{2,1,0:T(4,128)} %get-tuple-element.41), channel_id=1, source_target_pairs={{0,8},{8,16},{16,24},{1,9},{9,17},{17,25},{2,10},{10,18},{18,26},{... | collective-permute-start | bytes 983048 | tf_op jit(solution)/shard_map/ppermute | solution.py:20
  165.8 29.6 %collective-permute-start.11 = (f32[80,4,256]{2,1,0:T(4,128)}, f32[80,4,256]{2,1,0:T(4,128)}, u32[]{:S(2)}, u32[]{:S(2)}) collective-permute-start(f32[80,4,256]{2,1,0:T(4,128)} %get-tuple-element.42), channel_id=1, source_target_pairs={{8,0},{16,8},{24,16},{9,1},{17,9},{25,17},{10,2},{18,10},{26,18},{... | collective-permute-start | bytes 983048 | tf_op jit(solution)/shard_map/ppermute | solution.py:21
  167.9 4.9 %copy-start.4 = (f32[80,16,256]{2,1,0:T(8,128)S(1)}, f32[80,16,256]{2,1,0:T(8,128)}, u32[]{:S(2)}) copy-start(f32[80,16,256]{2,1,0:T(8,128)} %get-tuple-element.52) | copy-start | bytes 3932164
  185.7 8.9 %collective-permute-start.14 = (f32[80,16,4]{0,1,2:T(8,128)S(1)}, f32[80,16,4]{0,1,2:T(8,128)S(1)}, u32[]{:S(2)}, u32[]{:S(2)}) collective-permute-start(f32[80,16,4]{0,1,2:T(8,128)S(1)} %copy.55), channel_id=1, source_target_pairs={{0,1},{1,2},{2,3},{3,4},{4,5},{5,6},{6,7},{8,9},{9,10},{10,11},{11... | collective-permute-start | bytes 61448 | tf_op jit(solution)/shard_map/ppermute | solution.py:20
  188.6 6.4 %collective-permute-start.15 = (f32[80,16,4]{0,1,2:T(8,128)S(1)}, f32[80,16,4]{0,1,2:T(8,128)S(1)}, u32[]{:S(2)}, u32[]{:S(2)}) collective-permute-start(f32[80,16,4]{0,1,2:T(8,128)S(1)} %copy.57), channel_id=1, source_target_pairs={{1,0},{2,1},{3,2},{4,3},{5,4},{6,5},{7,6},{9,8},{10,9},{11,10},{12... | collective-permute-start | bytes 61448 | tf_op jit(solution)/shard_map/ppermute | solution.py:21
  195.4 16.7 %copy-start.16 = (f32[80,16,256]{2,1,0:T(8,128)S(1)}, f32[80,16,256]{2,1,0:T(8,128)}, u32[]{:S(2)}) copy-start(f32[80,16,256]{2,1,0:T(8,128)} %param.19) | copy-start | bytes 3932164
  195.4 16.7 %copy-start.15 = (f32[2,80,16,256]{3,2,1,0:T(8,128)S(1)}, f32[2,80,16,256]{3,2,1,0:T(8,128)}, u32[]{:S(2)}) copy-start(f32[2,80,16,256]{3,2,1,0:T(8,128)} %param.18) | copy-start | bytes 7864324
  212.1 1.9 copy-start.8
  212.1 1.9 copy-start.1
where the time goes:
time: 218 us; the launch traced here: 214 us
  other arithmetic  110 us (50%)
  starting transfers between devices  55.7 us (26%)
  local copies, waits for them, and re-layouts  33.5 us (15%)
  waiting for transfers between devices  12.6 us (6%)
    ppermute x8, starting transfers between devices, extended(): before = lax.ppermute(last, axis, up)  34.4 us
    sub x2, other arithmetic, local(): press = press - kappa * diverge  32.8 us
    scatter-add x1, other arithmetic, local(): jnp.zeros((steps, plane_cells + 1), jnp.float32).at[:, cells].add(sources)  13.7 us
    sub x2, other arithmetic, local(): vel_x = vel_x - buoyancy[0] * plus_diff(padded[:, :, 4:4 + cy], 1, cx)  13.3 us
    unnamed x1, other arithmetic  11.8 us
    sub x1, other arithmetic, local(): vel_y = vel_y - buoyancy[1] * plus_diff(padded[:, 4:4 + cx, :], 2, cy)  11.1 us
    ppermute x8, starting transfers between devices, extended(): after = lax.ppermute(initial, axis, down)  10.6 us
    ppermute x8, waiting for transfers between devices, extended(): after = lax.ppermute(initial, axis, down)  10.5 us
  transfers between devices with their start and end apart: 18, of which 4 were waited for; matrix products, arithmetic and copies ran while one was open for 35% of the time, Pallas kernels for 0%

commit v1 on v0

v1 whole, which is shorter than its diff:
```python
import functools

import jax
import jax.numpy as jnp
import ml_dtypes
import numpy as np
from jax import lax
from jax.experimental import pallas as pl
from jax.experimental.pallas import tpu as pltpu
from jax.sharding import PartitionSpec as P

STEPS = 2
REC_DEPTH = 3
ZC = 16
MESH = pl.DeviceIdType.MESH
F32 = jnp.float32
BF16 = jnp.bfloat16

coeffs = (1225.0 / 1024.0, -245.0 / 3072.0, 49.0 / 5120.0, -5.0 / 7168.0)


def tap(offset, plus):
    for k in range(1, 5):
        if offset == (k if plus else k - 1):
            return coeffs[k - 1]
        if offset == (1 - k if plus else -k):
            return -coeffs[k - 1]
    return 0.0


def band(outs, ins, plus):
    return np.array([[tap(i - o, plus) for i in ins] for o in outs], np.float64)


def parts(m):
    m = np.asarray(m, np.float32)
    hi = m.astype(ml_dtypes.bfloat16)
    lo = (m - hi.astype(np.float32)).astype(ml_dtypes.bfloat16)
    return hi, lo


def x_matrix(cx, plus):
    eye = np.eye(ZC)
    low, up = (3, 4) if plus else (4, 3)
    own = np.kron(eye, band(range(cx), range(cx), plus))
    below = np.kron(eye, band(range(cx), range(-low, 0), plus))
    above = np.kron(eye, band(range(cx), range(cx, cx + up), plus))
    oh, ol = parts(own)
    hh, hl = parts(np.concatenate([below, above], axis=1))
    pad = np.zeros((ZC * cx, 48), ml_dtypes.bfloat16)
    return np.concatenate([oh, oh, ol, hh, hh, hl, pad], axis=1)


def y_matrix(cy, plus):
    own = band(range(cy), range(cy), plus).T
    halo = band(range(cy), list(range(-8, 0)) + list(range(cy, cy + 8)), plus).T
    oh, ol = parts(own)
    hh, hl = parts(halo)
    pad = np.zeros((80, cy), ml_dtypes.bfloat16)
    return np.concatenate([oh, oh, ol, hh, hh, hl, pad], axis=0)


def x_edges(cx, plus):
    low, up = (3, 4) if plus else (4, 3)
    eye = np.eye(ZC)
    to_up = np.kron(eye, np.eye(cx)[cx - low:])
    to_low = np.kron(eye, np.eye(cx)[:up])
    pick = np.concatenate([to_up, to_low], axis=0).astype(ml_dtypes.bfloat16)
    return np.concatenate([pick, pick], axis=1)


def y_edges(cy):
    eye = np.eye(cy)
    pick = np.concatenate([eye[cy - 8:], eye[:8]], axis=0).astype(ml_dtypes.bfloat16)
    return np.concatenate([pick, pick], axis=1)


def split(v):
    hi = v.astype(BF16)
    return hi, (v - hi.astype(F32)).astype(BF16)


def dot(a, b):
    return lax.dot_general(a, b, (((1,), (0,)), ((), ())), preferred_element_type=F32)


def dot_nt(a, b):
    return lax.dot_general(a, b, (((1,), (1,)), ((), ())), preferred_element_type=F32)


def route_kernel(devices, slots, traces_ref, kernel_ref, tile_ref, cell_ref, out_ref):
    rows = traces_ref.shape[0]
    src = lax.dot_general(
        kernel_ref[...], traces_ref[...], (((1,), (1,)), ((), ())),
        precision=lax.Precision.HIGHEST, preferred_element_type=F32)
    tiles = tile_ref[...]
    cells = cell_ref[...]
    named = lax.broadcasted_iota(jnp.int32, (devices, rows), 0) == tiles
    onehot = jnp.where(named, 1.0, 0.0)
    earlier = (lax.broadcasted_iota(jnp.int32, (rows, rows), 0)
               < lax.broadcasted_iota(jnp.int32, (rows, rows), 1))
    count = dot(onehot.astype(BF16), jnp.where(earlier, 1.0, 0.0).astype(BF16))
    rank = jnp.sum(count * onehot, axis=0, keepdims=True)
    slot_id = lax.broadcasted_iota(jnp.int32, (slots, rows), 0).astype(F32)
    place = jnp.where(slot_id == rank, 1.0, 0.0).astype(BF16)
    hi = src.astype(BF16).astype(F32)
    lo = src - hi
    cell_x = (cells // 256).astype(F32)
    cell_y = (cells % 256).astype(F32)
    vals = [hi[0:1], lo[0:1], hi[1:2], lo[1:2], cell_x, cell_y]
    lhs = jnp.concatenate([(onehot * v).astype(BF16) for v in vals], axis=0)
    packed = dot_nt(lhs, place)
    d = devices
    out_ref[0] = packed[0:d] + packed[d:2 * d]
    out_ref[1] = packed[2 * d:3 * d] + packed[3 * d:4 * d]
    out_ref[2] = packed[4 * d:5 * d] * 256.0 + packed[5 * d:6 * d]


def step_kernel(n_tx, n_ty, nz, cx, cy,
                p_in, v_in, kap_in, b_in, fwd_in, g_in, recv_in,
                xp_in, xm_in, yp_in, ym_in, sxp_in, sxm_in, sy_in,
                p_out, v_out, g_out,
                p, vx, vy, vz, kap, buo, fwd, grad,
                xp, xm, yp, ym, sxp, sxm, sy,
                xs, xr, ys, yr, inj,
                in_sem, out_sem, send_sem, recv_sem):
    tx, ty = lax.axis_index("tx"), lax.axis_index("ty")
    rows = nz * cx
    cr = ZC * cx
    pad = 4 * cx
    n_chunks = rows // cr
    has = (tx < n_tx - 1, tx > 0, ty < n_ty - 1, ty > 0)
    ids = ({"tx": tx + 1}, {"tx": tx - 1}, {"ty": ty + 1}, {"ty": ty - 1})
    back = (1, 0, 3, 2)

    body = pl.ds(pad, rows)
    loads = [
        pltpu.make_async_copy(p_in, p.at[body], in_sem.at[0]),
        pltpu.make_async_copy(sxp_in, sxp, in_sem.at[1]),
        pltpu.make_async_copy(sy_in, sy, in_sem.at[2]),
        pltpu.make_async_copy(xp_in, xp, in_sem.at[3]),
        pltpu.make_async_copy(yp_in, yp, in_sem.at[4]),
        pltpu.make_async_copy(v_in.at[0], vx, in_sem.at[5]),
        pltpu.make_async_copy(v_in.at[1], vy, in_sem.at[6]),
        pltpu.make_async_copy(v_in.at[2], vz.at[body], in_sem.at[7]),
        pltpu.make_async_copy(b_in, buo, in_sem.at[8]),
        pltpu.make_async_copy(sxm_in, sxm, in_sem.at[9]),
        pltpu.make_async_copy(xm_in, xm, in_sem.at[10]),
        pltpu.make_async_copy(ym_in, ym, in_sem.at[11]),
        pltpu.make_async_copy(kap_in, kap, in_sem.at[12]),
        pltpu.make_async_copy(fwd_in, fwd, in_sem.at[13]),
        pltpu.make_async_copy(g_in, grad, in_sem.at[14]),
    ]
    for copy in loads:
        copy.start()

    zeros = jnp.zeros((pad, cy), F32)
    for ref in (p, vz):
        ref[0:pad, :] = zeros
        ref[pad + rows:, :] = zeros

    def span(ph, d):
        low, up = (3 * ZC, 4 * ZC) if ph % 2 == 0 else (4 * ZC, 3 * ZC)
        return ((0, low), (low, up), (0, 8), (8, 8))[d]

    def clear(d):
        @pl.when(jnp.logical_not(has[back[d]]))
        def _():
            for ph in range(4):
                start, size = span(ph, d)
                ref = xr if d < 2 else yr
                for c in range(n_chunks):
                    ref[ph, c, start:start + size, :] = jnp.zeros((size, ref.shape[3]), F32)

    for d in range(4):
        clear(d)

    barrier = pltpu.get_barrier_semaphore()
    for d in range(4):
        @pl.when(has[d])
        def _(d=d):
            pl.semaphore_signal(barrier, inc=1, device_id=ids[d], device_id_type=MESH)
    peers = sum(h.astype(jnp.int32) for h in has)
    pl.semaphore_wait(barrier, peers)

    def halo_copy(ph, c, d):
        start, size = span(ph, d)
        src, dst = (xs, xr) if d < 2 else (ys, yr)
        return pltpu.make_async_remote_copy(
            src_ref=src.at[ph, c, pl.ds(start, size)],
            dst_ref=dst.at[ph, c, pl.ds(start, size)],
            send_sem=send_sem.at[ph, c, d],
            recv_sem=recv_sem.at[ph, c, d],
            device_id=ids[d], device_id_type=MESH)

    def send(ph, c):
        for d in range(4):
            @pl.when(has[d])
            def _(d=d):
                halo_copy(ph, c, d).start()

    def arrive(ph, c):
        for d in range(4):
            @pl.when(has[back[d]])
            def _(d=d):
                start, size = span(ph, d)
                src, dst = (xs, xr) if d < 2 else (ys, yr)
                pltpu.make_async_remote_copy(
                    src_ref=src.at[ph, c, pl.ds(start, size)],
                    dst_ref=dst.at[ph, c, pl.ds(start, size)],
                    send_sem=send_sem.at[ph, c, d],
                    recv_sem=recv_sem.at[ph, c, d],
                    device_id=ids[back[d]], device_id_type=MESH).wait_recv()

    def post(ph, c, pick, fx, fy):
        hi, lo = split(fx)
        xs[ph, c] = dot(pick[...], jnp.concatenate([hi, lo], axis=0))
        hi, lo = split(fy)
        ys[ph, c] = dot_nt(sy[...], jnp.concatenate([hi, lo], axis=1))
        send(ph, c)

    def x_diff(ph, c, field, matrix):
        hi, lo = split(field)
        hh, hl = split(xr[ph, c])
        tail = jnp.zeros((48, cy), BF16)
        return dot(matrix[...], jnp.concatenate([hi, lo, hi, hh, hl, hh, tail], axis=0))

    def y_diff(ph, c, field, matrix):
        hi, lo = split(field)
        hh, hl = split(yr[ph, c])
        hh, hl = hh.astype(F32), hl.astype(F32)
        halo = jnp.concatenate([hh, hl, hh, jnp.zeros((80, cr), F32)], axis=0)
        return dot(jnp.concatenate([hi, lo, hi, halo.T.astype(BF16)], axis=1), matrix[...])

    def z_diff(ref, c, plus):
        total = None
        for k in range(1, 5):
            a, b = (k, 1 - k) if plus else (k - 1, -k)
            fa = ref[pl.ds(pl.multiple_of(c * cr + (pad + a * cx), 8), cr), :]
            fb = ref[pl.ds(pl.multiple_of(c * cr + (pad + b * cx), 8), cr), :]
            term = coeffs[k - 1] * (fa - fb)
            total = term if total is None else total + term
        return total

    def at(c):
        return pl.ds(pl.multiple_of(c * cr, cr), cr)

    def padded_at(c):
        return pl.ds(pl.multiple_of(c * cr + pad, 8), cr)

    for i in range(3):
        loads[i].wait()

    @pl.loop(0, n_chunks)
    def _(c):
        f = p[padded_at(c), :]
        post(0, c, sxp, f, f)

    slots_all = recv_in.shape[1]
    piece = 512
    total = jnp.zeros((4 * cx, cy), F32)
    for r in range(slots_all // piece):
        got = recv_in[:, r * piece:(r + 1) * piece]
        cell = got[2:3].astype(jnp.int32)
        at_x = lax.broadcasted_iota(jnp.int32, (cx, piece), 0) == cell // cy
        at_y = lax.broadcasted_iota(jnp.int32, (cy, piece), 0) == cell % cy
        pieces = []
        for s in range(STEPS):
            v = got[s:s + 1]
            hi = v.astype(BF16).astype(F32)
            pieces.append(jnp.where(at_x, hi, 0.0).astype(BF16))
            pieces.append(jnp.where(at_x, v - hi, 0.0).astype(BF16))
        total = total + dot_nt(jnp.concatenate(pieces, axis=0),
                               jnp.where(at_y, 1.0, 0.0).astype(BF16))
    for s in range(STEPS):
        inj[s] = total[2 * s * cx:(2 * s + 1) * cx] + total[(2 * s + 1) * cx:(2 * s + 2) * cx]

    for i in range(3, 10):
        loads[i].wait()

    for s in range(STEPS):
        @pl.loop(0, n_chunks)
        def _(c, s=s):
            vz[padded_at(c), :] = vz[padded_at(c), :] - buo[2, at(c), :] * z_diff(p, c, True)
            arrive(2 * s, c)
            f = p[padded_at(c), :]
            nx = vx[at(c), :] - buo[0, at(c), :] * x_diff(2 * s, c, f, xp)
            vx[at(c), :] = nx
            ny = vy[at(c), :] - buo[1, at(c), :] * y_diff(2 * s, c, f, yp)
            vy[at(c), :] = ny
            post(2 * s + 1, c, sxm, nx, ny)

        if s == 0:
            for i in range(10, 15):
                loads[i].wait()
        if s == STEPS - 1:
            outs = [
                pltpu.make_async_copy(vx, v_out.at[0], out_sem.at[0]),
                pltpu.make_async_copy(vy, v_out.at[1], out_sem.at[1]),
                pltpu.make_async_copy(vz.at[body], v_out.at[2], out_sem.at[2]),
            ]
            for copy in outs:
                copy.start()

        @pl.loop(0, n_chunks)
        def _(c, s=s):
            dz = z_diff(vz, c, False)
            arrive(2 * s + 1, c)
            div = (x_diff(2 * s + 1, c, vx[at(c), :], xm)
                   + y_diff(2 * s + 1, c, vy[at(c), :], ym) + dz)
            p[padded_at(c), :] = p[padded_at(c), :] - kap[at(c), :] * div

            @pl.when(c == REC_DEPTH // ZC)
            def _():
                row = pad + REC_DEPTH * cx
                p[row:row + cx, :] = p[row:row + cx, :] + inj[s]

            f = p[padded_at(c), :]
            grad[at(c), :] = grad[at(c), :] + fwd[s, at(c), :] * f
            if s < STEPS - 1:
                post(2 * s + 2, c, sxp, f, f)

    last = [
        pltpu.make_async_copy(p.at[body], p_out, out_sem.at[3]),
        pltpu.make_async_copy(grad, g_out, out_sem.at[4]),
    ]
    for copy in last:
        copy.start()

    @pl.loop(0, n_chunks)
    def _(c):
        for ph in range(4):
            for d in range(4):
                @pl.when(has[d])
                def _(ph=ph, d=d):
                    halo_copy(ph, c, d).wait_send()

    for copy in outs + last:
        copy.wait()


def local(
    pressure, velocity, kappa, buoyancy, fwd_pressure, gradient, traces, kernel, rec_tile, rec_cell
):
    nz, cx, cy = pressure.shape
    n_rows, samples = traces.shape
    n_tx, n_ty = lax.axis_size("tx"), lax.axis_size("ty")
    devices = n_tx * n_ty
    slots = max(4, 2 * n_rows // devices)
    vmem = pl.BlockSpec(memory_space=pltpu.VMEM)
    anywhere = pl.BlockSpec(memory_space=pl.ANY)

    packed = pl.pallas_call(
        functools.partial(route_kernel, devices, slots),
        out_shape=jax.ShapeDtypeStruct((3, devices, slots), F32),
        in_specs=[vmem] * 4,
        out_specs=vmem,
        compiler_params=pltpu.CompilerParams(vmem_limit_bytes=32 * 2**20),
        name="route",
    )(traces, kernel, rec_tile.reshape(1, n_rows), rec_cell.reshape(1, n_rows))
    got = lax.all_to_all(packed, ("tx", "ty"), split_axis=1, concat_axis=1, tiled=True)
    got = got.reshape(3, devices * slots)

    rows = nz * cx
    cr = ZC * cx
    nc = rows // cr
    pad = 4 * cx
    flat = lambda a: a.reshape(a.shape[:-3] + (rows, cy))
    mats = [x_matrix(cx, True), x_matrix(cx, False), y_matrix(cy, True), y_matrix(cy, False),
            x_edges(cx, True), x_edges(cx, False), y_edges(cy)]
    field = lambda *lead: pltpu.VMEM(lead + (rows, cy), F32)
    press, vel, grad = pl.pallas_call(
        functools.partial(step_kernel, n_tx, n_ty, nz, cx, cy),
        out_shape=(jax.ShapeDtypeStruct((rows, cy), F32),
                   jax.ShapeDtypeStruct((3, rows, cy), F32),
                   jax.ShapeDtypeStruct((rows, cy), F32)),
        in_specs=[anywhere] * 6 + [vmem] + [anywhere] * 7,
        out_specs=(anywhere,) * 3,
        scratch_shapes=[
            pltpu.VMEM((rows + 2 * pad, cy), F32), field(), field(),
            pltpu.VMEM((rows + 2 * pad, cy), F32), field(), field(3), field(STEPS), field(),
        ] + [pltpu.VMEM(m.shape, BF16) for m in mats] + [
            pltpu.VMEM((4, nc, 7 * ZC, cy), F32), pltpu.VMEM((4, nc, 7 * ZC, cy), F32),
            pltpu.VMEM((4, nc, 16, cr), F32), pltpu.VMEM((4, nc, 16, cr), F32),
            pltpu.VMEM((STEPS, cx, cy), F32),
            pltpu.SemaphoreType.DMA((15,)), pltpu.SemaphoreType.DMA((5,)),
            pltpu.SemaphoreType.DMA((4, nc, 4)), pltpu.SemaphoreType.DMA((4, nc, 4)),
        ],
        compiler_params=pltpu.CompilerParams(
            collective_id=0, has_side_effects=True, vmem_limit_bytes=48 * 2**20),
        name="steps",
    )(flat(pressure), flat(velocity), flat(kappa), flat(buoyancy), flat(fwd_pressure),
      flat(gradient), got, *[jnp.asarray(m) for m in mats])
    return (press.reshape(nz, cx, cy), vel.reshape(3, nz, cx, cy), grad.reshape(nz, cx, cy))


def solution(mesh):
    return jax.shard_map(
        local,
        mesh=mesh,
        in_specs=(
            P(None, "tx", "ty"),
            P(None, None, "tx", "ty"),
            P(None, "tx", "ty"),
            P(None, None, "tx", "ty"),
            P(None, None, "tx", "ty"),
            P(None, "tx", "ty"),
            P(("tx", "ty"), None),
            P(),
            P(("tx", "ty"), None),
            P(("tx", "ty")),
        ),
        out_specs=(P(None, "tx", "ty"), P(None, None, "tx", "ty"), P(None, "tx", "ty")),
        check_vma=False,
    )
```

time: 218 us -> 86.7 us (0.40); the launches traced: 214 us -> 86.3 us
  other arithmetic: 110 us -> 0.72 us
  Pallas kernels: 0 us -> 57.2 us
  starting transfers between devices: 55.7 us -> 0 us
  local copies, waits for them, and re-layouts: 33.5 us -> 13.3 us
  blocking collectives: 0 us -> 14.3 us
  waiting for transfers between devices: 12.6 us -> 0 us
    sub x6 -> x0, other arithmetic: 57.3 us -> none  [the longest x2 32.8 us: local(): press = press - kappa * diverge]
    pallas_call x0 -> x2, Pallas kernels: none -> 57.2 us  [the longest x1 55.8 us: local(): pl.pallas_call(functools.partial(step_kernel, n_tx, n_ty, nz, cx, cy), ou...]
    ppermute x16 -> x0, starting transfers between devices: 45 us -> none  [the longest x8 34.4 us: extended(): before = lax.ppermute(last, axis, up)]
    all_to_all x0 -> x1, blocking collectives: none -> 14.3 us  [local(): lax.all_to_all(packed, ('tx', 'ty'), split_axis=1, concat_axis=1, tiled=T...]
    scatter-add x3 -> x0, other arithmetic: 13.7 us -> none  [the longest x1 13.7 us: local(): jnp.zeros((steps, plane_cells + 1), jnp.float32).at[:, cells].add(sources)]
    slice x17 -> x0, local copies, waits for them, and re-layouts: 13.6 us -> none  [the longest x10 9.34 us: extended(): last = lax.slice_in_dim(value, length - width, length, axis=dim)]
    another operation x3 -> x0, other arithmetic: 13.5 us -> none
    unnamed x1 -> x0, other arithmetic: 11.8 us -> none
  transfers between devices with their start and end apart: 18 -> 0, of which waited for: 4 -> 0; matrix products, arithmetic and copies ran while one was open for 35% -> 0% of each run, Pallas kernels for 0% -> 0%
where the time goes in v1:
time: 86.7 us; the launch traced here: 86.3 us
  Pallas kernels  57.2 us (66%)
  blocking collectives  14.3 us (16%)
  local copies, waits for them, and re-layouts  13.3 us (15%)
    pallas_call x1, Pallas kernels, local(): pl.pallas_call(functools.partial(step_kernel, n_tx, n_ty, nz, cx, cy), ou...  55.8 us
    all_to_all x1, blocking collectives, local(): lax.all_to_all(packed, ('tx', 'ty'), split_axis=1, concat_axis=1, tiled=T...  14.3 us
    unnamed x27, local copies, waits for them, and re-layouts  12.7 us

profile of v1, /device:TPU:0, one launch (start us, length us, event | category | flops | bytes accessed | tf_op | source)
XLA Modules:
  0.0 86.3 jit_solution(15961283771619805017)
XLA Ops:
  0.6 0.0 copy-start
  0.6 1.2 %copy-done = f32[1024,256]{1,0:T(8,128)S(1)} copy-done((f32[1024,256]{1,0:T(8,128)S(1)}, f32[1024,256]{1,0:T(8,128)}, u32[]{:S(2)}) %copy-start) | copy-done | bytes 1048600
  1.9 0.0 copy-start.8
  1.9 0.7 copy-done.8
  2.5 0.0 copy-start.9
  2.5 0.7 copy-done.9
  3.2 0.0 copy-start.10
  3.2 0.7 copy-done.10
  3.9 0.0 copy-start.1
  3.9 0.0 copy-start.2
  3.9 0.0 copy-start.3
  3.9 0.0 copy-start.5
  3.9 1.4 %route.1 = f32[3,32,64]{2,1,0:T(8,128)S(1)} custom-call(f32[1024,256]{1,0:T(8,128)S(1)} %copy-done, f32[2,256]{1,0:T(2,128)S(1)} %copy-done.10, s32[1,1024]{1,0:T(1,128)S(1)} %bitcast.17, s32[1,1024]{1,0:T(1,128)S(1)} %bitcast.18), custom_call_target="tpu_custom_call" | custom-call | tf_op jit(solution)/shard_map/route/pallas_call | solution.py:353
  5.4 0.1 reshape.54
  5.5 14.3 %all_to_all.5 = f32[32,1,192]{2,1,0:T(1,128)S(1)} all-to-all(f32[32,1,192]{2,1,0:T(1,128)S(1)} %reshape.54), channel_id=1, replica_groups=mesh['tx'=4,'ty'=8] {'tx','ty'}, dimensions={0} | all-to-all | bytes 49152 | tf_op jit(solution)/shard_map/all_to_all | solution.py:361
  19.9 0.5 broadcast
  20.4 0.7 reduce
  21.1 0.1 reshape.55
  21.2 0.1 reshape.50.recv_in
  21.3 0.0 copy-done.1
  21.3 0.0 copy-done.2
  21.3 0.0 copy-done.3
  21.3 0.0 copy-done.5
  21.3 0.0 copy-start.4
  21.4 1.0 %copy-done.4 = bf16[896,256]{1,0:T(8,128)(2,1)S(1)} copy-done((bf16[896,256]{1,0:T(8,128)(2,1)S(1)}, bf16[896,256]{1,0:T(8,128)(2,1)}, u32[]{:S(2)}) %copy-start.4) | copy-done | bytes 458776
  22.4 0.0 copy-start.6
  22.4 0.9 %copy-done.6 = bf16[112,512]{1,0:T(8,128)(2,1)S(1)} copy-done((bf16[112,512]{1,0:T(8,128)(2,1)S(1)}, bf16[112,512]{1,0:T(8,128)(2,1)}, u32[]{:S(2)}) %copy-start.6) | copy-done | bytes 114712
  23.3 0.0 copy-start.7
  23.3 0.7 copy-done.7
  24.0 55.8 %steps.1 = (f32[1280,256]{1,0:T(8,128)S(1)}, f32[3,1280,256]{2,1,0:T(8,128)}, f32[1280,256]{1,0:T(8,128)S(1)}) custom-call(f32[1280,256]{1,0:T(8,128)} %bitcast.23, f32[3,1280,256]{2,1,0:T(8,128)} %bitcast.19, f32[1280,256]{1,0:T(8,128)} %bitcast.24, f32[3,1280,256]{2,1,0:T(8,128)} %bitcast.20, f32[2,1280,256]{2,1,0:T(8,128)} %bitcast.22, ...), custom_call_target="tpu_custom_call" | custom-call | tf_op jit(solution)/shard_map/steps/pallas_call | solution.py:372
  79.8 1.1 %copy.27 = f32[80,16,256]{2,1,0:T(8,128)} copy(f32[80,16,256]{2,1,0:T(8,128)S(1)} %bitcast.16) | data formatting | bytes 2621440
  80.8 4.4 %copy.28 = f32[3,80,16,256]{3,2,1,0:T(8,128)} copy(f32[3,80,16,256]{3,2,1,0:T(8,128)} %bitcast.21) | data formatting | bytes 7864320
  85.3 1.1 %copy.29 = f32[80,16,256]{2,1,0:T(8,128)} copy(f32[80,16,256]{2,1,0:T(8,128)S(1)} %bitcast.15) | data formatting | bytes 2621440
  (2 shorter events, 0.0 us)
Async XLA Ops:
  0.6 1.2 %copy-start = (f32[1024,256]{1,0:T(8,128)S(1)}, f32[1024,256]{1,0:T(8,128)}, u32[]{:S(2)}) copy-start(f32[1024,256]{1,0:T(8,128)} %traces_ref.1) | copy-start | bytes 3145732
  1.9 0.7 copy-start.8
  2.5 0.7 copy-start.9
  3.2 0.7 copy-start.10
  3.9 17.4 %copy-start.1 = (bf16[256,1152]{1,0:T(8,128)(2,1)S(1)}, bf16[256,1152]{1,0:T(8,128)(2,1)}, u32[]{:S(2)}) copy-start(bf16[256,1152]{1,0:T(8,128)(2,1)} %constant.15.clone.xm_in) | copy-start | bytes 1769476
  3.9 17.4 %copy-start.2 = (bf16[256,1152]{1,0:T(8,128)(2,1)S(1)}, bf16[256,1152]{1,0:T(8,128)(2,1)}, u32[]{:S(2)}) copy-start(bf16[256,1152]{1,0:T(8,128)(2,1)} %constant.14.clone.xp_in) | copy-start | bytes 1769476
  3.9 17.4 %copy-start.3 = (bf16[896,256]{1,0:T(8,128)(2,1)S(1)}, bf16[896,256]{1,0:T(8,128)(2,1)}, u32[]{:S(2)}) copy-start(bf16[896,256]{1,0:T(8,128)(2,1)} %constant.17.clone.ym_in) | copy-start | bytes 1376260
  3.9 17.4 %copy-start.5 = (bf16[112,512]{1,0:T(8,128)(2,1)S(1)}, bf16[112,512]{1,0:T(8,128)(2,1)}, u32[]{:S(2)}) copy-start(bf16[112,512]{1,0:T(8,128)(2,1)} %constant.19.clone.sxm_in) | copy-start | bytes 344068
  21.3 1.0 %copy-start.4 = (bf16[896,256]{1,0:T(8,128)(2,1)S(1)}, bf16[896,256]{1,0:T(8,128)(2,1)}, u32[]{:S(2)}) copy-start(bf16[896,256]{1,0:T(8,128)(2,1)} %constant.16.clone.yp_in) | copy-start | bytes 1376260
  22.4 0.9 %copy-start.6 = (bf16[112,512]{1,0:T(8,128)(2,1)S(1)}, bf16[112,512]{1,0:T(8,128)(2,1)}, u32[]{:S(2)}) copy-start(bf16[112,512]{1,0:T(8,128)(2,1)} %constant.18.clone.sxp_in) | copy-start | bytes 344068
  23.3 0.7 copy-start.7

commit v2 on v1

v2 whole, which is shorter than its diff:
```python
import functools

import jax
import jax.numpy as jnp
import ml_dtypes
import numpy as np
from jax import lax
from jax.experimental import pallas as pl
from jax.experimental.pallas import tpu as pltpu
from jax.sharding import PartitionSpec as P

STEPS = 2
REC_DEPTH = 3
ZC = 16
MESH = pl.DeviceIdType.MESH
F32 = jnp.float32
BF16 = jnp.bfloat16

coeffs = (1225.0 / 1024.0, -245.0 / 3072.0, 49.0 / 5120.0, -5.0 / 7168.0)


def tap(offset, plus):
    for k in range(1, 5):
        if offset == (k if plus else k - 1):
            return coeffs[k - 1]
        if offset == (1 - k if plus else -k):
            return -coeffs[k - 1]
    return 0.0


def taps(offset, plus):
    hi = jnp.zeros(offset.shape, F32)
    lo = jnp.zeros(offset.shape, F32)
    for at in range(-4, 5):
        c = tap(at, plus)
        if c != 0.0:
            c_hi = float(np.float32(c).astype(ml_dtypes.bfloat16))
            hi = jnp.where(offset == at, c_hi, hi)
            lo = jnp.where(offset == at, float(np.float32(c)) - c_hi, lo)
    return hi, lo


def grid_of(shape):
    return (lax.broadcasted_iota(jnp.int32, shape, 0), lax.broadcasted_iota(jnp.int32, shape, 1))


FAR = 1 << 20


def build_x(ref, cx, plus):
    cr = ZC * cx
    low = 3 if plus else 4
    row, col = grid_of((cr, cr))
    hi, lo = taps(jnp.where(row // cx == col // cx, col % cx - row % cx, FAR), plus)
    ref[:, 0:cr] = hi.astype(BF16)
    ref[:, cr:2 * cr] = hi.astype(BF16)
    ref[:, 2 * cr:3 * cr] = lo.astype(BF16)
    width = 7 * ZC
    row, col = grid_of((cr, ref.shape[1] - 3 * cr))
    seg = jnp.where(col < width, 0, jnp.where(col < 2 * width, 1, jnp.where(col < 3 * width, 2, 3)))
    at = col - seg * width
    layer = at // ZC
    x = jnp.where(layer < low, layer - low, cx + layer - low)
    hi, lo = taps(jnp.where(row // cx == at % ZC, x - row % cx, FAR), plus)
    ref[:, 3 * cr:] = jnp.where(seg < 2, hi, jnp.where(seg == 2, lo, 0.0)).astype(BF16)


def build_y(ref, cy, plus):
    row, col = grid_of((cy, cy))
    hi, lo = taps(row - col, plus)
    ref[0:cy] = hi.astype(BF16)
    ref[cy:2 * cy] = hi.astype(BF16)
    ref[2 * cy:3 * cy] = lo.astype(BF16)
    row, col = grid_of((ref.shape[0] - 3 * cy, cy))
    seg, at = row // 16, row % 16
    hi, lo = taps(jnp.where(at < 8, at - 8, cy + at - 8) - col, plus)
    ref[3 * cy:] = jnp.where(seg < 2, hi, jnp.where(seg == 2, lo, 0.0)).astype(BF16)


def build_x_edges(ref, cx, plus):
    low = 3 if plus else 4
    row, col = grid_of(ref.shape)
    at = col % (ZC * cx)
    layer = row // ZC
    x = jnp.where(layer < low, cx - low + layer, layer - low)
    ref[...] = jnp.where(at == (row % ZC) * cx + x, 1.0, 0.0).astype(BF16)


def build_y_edges(ref, cy):
    row, col = grid_of(ref.shape)
    ref[...] = jnp.where(col % cy == jnp.where(row < 8, cy - 8 + row, row - 8), 1.0, 0.0).astype(BF16)


def split(v):
    hi = v.astype(BF16)
    return hi, (v - hi.astype(F32)).astype(BF16)


def dot(a, b):
    return lax.dot_general(a, b, (((1,), (0,)), ((), ())), preferred_element_type=F32)


def dot_nt(a, b):
    return lax.dot_general(a, b, (((1,), (1,)), ((), ())), preferred_element_type=F32)


def pack(devices, traces, kernel, tiles, cells):
    rows = traces.shape[0]
    src = lax.dot_general(
        kernel, traces, (((1,), (1,)), ((), ())),
        precision=lax.Precision.HIGHEST, preferred_element_type=F32)
    named = lax.broadcasted_iota(jnp.int32, (devices, rows), 0) == tiles
    onehot = jnp.where(named, 1.0, 0.0)
    row, col = grid_of((rows, rows))
    count = dot(onehot.astype(BF16), jnp.where(row < col, 1.0, 0.0).astype(BF16))
    rank = jnp.sum(count * onehot, axis=0, keepdims=True)
    slot_id = lax.broadcasted_iota(jnp.int32, (128, rows), 0).astype(F32)
    place = jnp.where(slot_id == rank, 1.0, 0.0).astype(BF16)
    src_hi = src.astype(BF16).astype(F32)
    cell_lo = cells % 256
    none = jnp.zeros((5, rows), F32)
    hi = jnp.concatenate([src_hi, (cells - cell_lo).astype(F32), none], axis=0)
    lo = jnp.concatenate([src - src_hi, cell_lo.astype(F32), none], axis=0)
    packed = None
    for v in (hi, lo):
        spread = jnp.concatenate([v] * devices, axis=0)
        to = lax.broadcasted_iota(jnp.int32, (devices * 8, rows), 0) // 8 == tiles
        part = dot_nt(jnp.where(to, spread, 0.0).astype(BF16), place)
        packed = part if packed is None else packed + part
    return packed.reshape(devices, 8, 128)


def step_kernel(n_tx, n_ty, nz, cx, cy,
                p_in, v_in, kap_in, b_in, fwd_in, g_in, traces_in, kernel_in, tile_in, cell_in,
                p_out, v_out, g_out,
                p, vx, vy, vz, kap, buo, fwd, grad, traces, filt, tiles, cells,
                xp, xm, yp, ym, sxp, sxm, sy,
                xs, xr, ys, yr, ts, tr, inj,
                in_sem, out_sem, send_sem, recv_sem, to_sem, from_sem):
    tx, ty = lax.axis_index("tx"), lax.axis_index("ty")
    devices = n_tx * n_ty
    me = tx * n_ty + ty
    rows = nz * cx
    cr = ZC * cx
    pad = 4 * cx
    n_chunks = rows // cr
    has = (tx < n_tx - 1, tx > 0, ty < n_ty - 1, ty > 0)
    ids = ({"tx": tx + 1}, {"tx": tx - 1}, {"ty": ty + 1}, {"ty": ty - 1})
    back = (1, 0, 3, 2)

    body = pl.ds(pad, rows)
    pairs = [
        (p_in, p.at[body]), (traces_in, traces), (kernel_in, filt), (tile_in, tiles),
        (cell_in, cells), (v_in.at[0], vx), (v_in.at[1], vy), (v_in.at[2], vz.at[body]),
        (b_in, buo), (kap_in, kap), (fwd_in, fwd), (g_in, grad),
    ]
    loads = [pltpu.make_async_copy(a, b, in_sem.at[i]) for i, (a, b) in enumerate(pairs)]
    for copy in loads:
        copy.start()

    barrier = pltpu.get_barrier_semaphore()

    def peer(o):
        to = lax.rem(me + o, devices)
        return to, {"tx": to // n_ty, "ty": lax.rem(to, n_ty)}

    @pl.loop(1, devices)
    def _(o):
        pl.semaphore_signal(barrier, inc=1, device_id=peer(o)[1], device_id_type=MESH)

    zeros = jnp.zeros((pad, cy), F32)
    for ref in (p, vz):
        ref[0:pad, :] = zeros
        ref[pad + rows:, :] = zeros

    def span(ph, d):
        low, up = (3 * ZC, 4 * ZC) if ph % 2 == 0 else (4 * ZC, 3 * ZC)
        return ((0, low), (low, up), (0, 8), (8, 8))[d]

    def clear(d):
        @pl.when(jnp.logical_not(has[back[d]]))
        def _():
            for ph in range(4):
                start, size = span(ph, d)
                ref = xr if d < 2 else yr
                for c in range(n_chunks):
                    ref[ph, c, start:start + size, :] = jnp.zeros((size, ref.shape[3]), F32)

    for d in range(4):
        clear(d)

    build_x_edges(sxp, cx, True)
    build_y_edges(sy, cy)
    pl.semaphore_wait(barrier, devices - 1)

    def halo_copy(ph, c, d):
        start, size = span(ph, d)
        src, dst = (xs, xr) if d < 2 else (ys, yr)
        return pltpu.make_async_remote_copy(
            src_ref=src.at[ph, c, pl.ds(start, size)],
            dst_ref=dst.at[ph, c, pl.ds(start, size)],
            send_sem=send_sem.at[ph, c, d],
            recv_sem=recv_sem.at[ph, c, d],
            device_id=ids[d], device_id_type=MESH)

    def send(ph, c):
        for d in range(4):
            @pl.when(has[d])
            def _(d=d):
                halo_copy(ph, c, d).start()

    def arrive(ph, c):
        for d in range(4):
            @pl.when(has[back[d]])
            def _(d=d):
                start, size = span(ph, d)
                src, dst = (xs, xr) if d < 2 else (ys, yr)
                pltpu.make_async_remote_copy(
                    src_ref=src.at[ph, c, pl.ds(start, size)],
                    dst_ref=dst.at[ph, c, pl.ds(start, size)],
                    send_sem=send_sem.at[ph, c, d],
                    recv_sem=recv_sem.at[ph, c, d],
                    device_id=ids[back[d]], device_id_type=MESH).wait_recv()

    def post(ph, c, pick, fx, fy):
        hi, lo = split(fx)
        xs[ph, c] = dot(pick[...], jnp.concatenate([hi, lo], axis=0))
        hi, lo = split(fy)
        ys[ph, c] = dot_nt(sy[...], jnp.concatenate([hi, lo], axis=1))
        send(ph, c)

    def x_diff(ph, c, field, matrix):
        hi, lo = split(field)
        hh, hl = split(xr[ph, c])
        tail = jnp.zeros((48, cy), BF16)
        return dot(matrix[...], jnp.concatenate([hi, lo, hi, hh, hl, hh, tail], axis=0))

    def y_diff(ph, c, field, matrix):
        hi, lo = split(field)
        hh, hl = split(yr[ph, c])
        hh, hl = hh.astype(F32), hl.astype(F32)
        halo = jnp.concatenate([hh, hl, hh, jnp.zeros((80, cr), F32)], axis=0)
        return dot(jnp.concatenate([hi, lo, hi, halo.T.astype(BF16)], axis=1), matrix[...])

    def z_diff(ref, c, plus):
        total = None
        for k in range(1, 5):
            a, b = (k, 1 - k) if plus else (k - 1, -k)
            fa = ref[pl.ds(pl.multiple_of(c * cr + (pad + a * cx), 8), cr), :]
            fb = ref[pl.ds(pl.multiple_of(c * cr + (pad + b * cx), 8), cr), :]
            term = coeffs[k - 1] * (fa - fb)
            total = term if total is None else total + term
        return total

    def at(c):
        return pl.ds(pl.multiple_of(c * cr, cr), cr)

    def padded_at(c):
        return pl.ds(pl.multiple_of(c * cr + pad, 8), cr)

    loads[0].wait()

    @pl.loop(0, n_chunks)
    def _(c):
        f = p[padded_at(c), :]
        post(0, c, sxp, f, f)

    def trace_copy(o):
        to, place = peer(o)
        return pltpu.make_async_remote_copy(
            src_ref=ts.at[to], dst_ref=tr.at[o],
            send_sem=to_sem.at[o], recv_sem=from_sem.at[o],
            device_id=place, device_id_type=MESH)

    for i in range(1, 5):
        loads[i].wait()
    ts[...] = pack(devices, traces[...], filt[...], tiles[...], cells[...])

    @pl.loop(1, devices)
    def _(o):
        trace_copy(o).start()

    tr[0] = ts[me]
    build_x(xp, cx, True)
    build_y(yp, cy, True)
    build_x_edges(sxm, cx, False)
    for i in range(5, 9):
        loads[i].wait()

    def receive():
        @pl.loop(1, devices)
        def _(o):
            trace_copy(o).wait_recv()

        def gather(i, total):
            got = jnp.concatenate([tr[4 * i + j] for j in range(4)], axis=1)
            cell = got[2:3].astype(jnp.int32)
            at_x = lax.broadcasted_iota(jnp.int32, (cx, 512), 0) == cell // cy
            at_y = lax.broadcasted_iota(jnp.int32, (cy, 512), 0) == cell % cy
            pieces = []
            for s in range(STEPS):
                v = got[s:s + 1]
                hi = v.astype(BF16).astype(F32)
                pieces.append(jnp.where(at_x, hi, 0.0).astype(BF16))
                pieces.append(jnp.where(at_x, v - hi, 0.0).astype(BF16))
            return total + dot_nt(jnp.concatenate(pieces, axis=0),
                                  jnp.where(at_y, 1.0, 0.0).astype(BF16))

        total = lax.fori_loop(0, devices // 4, gather, jnp.zeros((4 * cx, cy), F32))
        for s in range(STEPS):
            inj[s] = total[2 * s * cx:(2 * s + 1) * cx] + total[(2 * s + 1) * cx:(2 * s + 2) * cx]

    for s in range(STEPS):
        @pl.loop(0, n_chunks)
        def _(c, s=s):
            nz_new = vz[padded_at(c), :] - buo[2, at(c), :] * z_diff(p, c, True)
            vz[padded_at(c), :] = nz_new
            arrive(2 * s, c)
            f = p[padded_at(c), :]
            nx = vx[at(c), :] - buo[0, at(c), :] * x_diff(2 * s, c, f, xp)
            vx[at(c), :] = nx
            ny = vy[at(c), :] - buo[1, at(c), :] * y_diff(2 * s, c, f, yp)
            vy[at(c), :] = ny
            post(2 * s + 1, c, sxm, nx, ny)

        if s == 0:
            build_x(xm, cx, False)
            build_y(ym, cy, False)
            receive()
            for i in range(9, 12):
                loads[i].wait()

        if s == STEPS - 1:
            outs = [
                pltpu.make_async_copy(vx, v_out.at[0], out_sem.at[0, 2]),
                pltpu.make_async_copy(vy, v_out.at[1], out_sem.at[1, 2]),
                pltpu.make_async_copy(vz.at[body], v_out.at[2], out_sem.at[2, 2]),
            ]
            for copy in outs:
                copy.start()

        def result(c):
            return (pltpu.make_async_copy(p.at[padded_at(c)], p_out.at[at(c)], out_sem.at[c, 0]),
                    pltpu.make_async_copy(grad.at[at(c)], g_out.at[at(c)], out_sem.at[c, 1]))

        @pl.loop(0, n_chunks)
        def _(c, s=s):
            dz = z_diff(vz, c, False)
            arrive(2 * s + 1, c)
            div = (x_diff(2 * s + 1, c, vx[at(c), :], xm)
                   + y_diff(2 * s + 1, c, vy[at(c), :], ym) + dz)
            p[padded_at(c), :] = p[padded_at(c), :] - kap[at(c), :] * div

            @pl.when(c == REC_DEPTH // ZC)
            def _():
                row = pad + REC_DEPTH * cx
                p[row:row + cx, :] = p[row:row + cx, :] + inj[s]

            f = p[padded_at(c), :]
            grad[at(c), :] = grad[at(c), :] + fwd[s, at(c), :] * f
            if s < STEPS - 1:
                post(2 * s + 2, c, sxp, f, f)
            else:
                for copy in result(c):
                    copy.start()

    @pl.loop(0, n_chunks)
    def _(c):
        for ph in range(4):
            for d in range(4):
                @pl.when(has[d])
                def _(ph=ph, d=d):
                    halo_copy(ph, c, d).wait_send()

    @pl.loop(1, devices)
    def _(o):
        trace_copy(o).wait_send()

    @pl.loop(0, n_chunks)
    def _(c):
        for copy in result(c):
            copy.wait()

    for copy in outs:
        copy.wait()


def hand_out(n_chunks, p_in, v_in, g_in, p_out, v_out, g_out, sem):
    rows = p_in.shape[0] // n_chunks
    copies = []
    for c in range(n_chunks):
        at = pl.ds(c * rows, rows)
        copies.append(pltpu.make_async_copy(p_in.at[at], p_out.at[at], sem.at[c, 0]))
        copies.append(pltpu.make_async_copy(g_in.at[at], g_out.at[at], sem.at[c, 1]))
        for i in range(3):
            copies.append(pltpu.make_async_copy(v_in.at[i, at], v_out.at[i, at], sem.at[c, 2 + i]))
    for copy in copies:
        copy.start()
    for copy in copies:
        copy.wait()


def local(
    pressure, velocity, kappa, buoyancy, fwd_pressure, gradient, traces, kernel, rec_tile, rec_cell
):
    nz, cx, cy = pressure.shape
    n_rows, samples = traces.shape
    n_tx, n_ty = lax.axis_size("tx"), lax.axis_size("ty")
    devices = n_tx * n_ty
    hbm = pl.BlockSpec(memory_space=pltpu.HBM)
    rows = nz * cx
    cr = ZC * cx
    nc = rows // cr
    pad = 4 * cx
    flat = lambda a: a.reshape(a.shape[:-3] + (rows, cy))
    field = lambda *lead: pltpu.VMEM(lead + (rows, cy), F32)
    half = lambda *shape: pltpu.VMEM(shape, BF16)
    dma = pltpu.SemaphoreType.DMA
    shapes = (jax.ShapeDtypeStruct((rows, cy), F32), jax.ShapeDtypeStruct((3, rows, cy), F32),
              jax.ShapeDtypeStruct((rows, cy), F32))
    results = pl.pallas_call(
        functools.partial(step_kernel, n_tx, n_ty, nz, cx, cy),
        out_shape=shapes,
        in_specs=[hbm] * 10,
        out_specs=(hbm,) * 3,
        scratch_shapes=[
            pltpu.VMEM((rows + 2 * pad, cy), F32), field(), field(),
            pltpu.VMEM((rows + 2 * pad, cy), F32), field(), field(3), field(STEPS), field(),
            pltpu.VMEM((n_rows, samples), F32), pltpu.VMEM(kernel.shape, F32),
            pltpu.VMEM((1, n_rows), jnp.int32), pltpu.VMEM((1, n_rows), jnp.int32),
            half(cr, 3 * cr + 384), half(cr, 3 * cr + 384),
            half(3 * cy + 128, cy), half(3 * cy + 128, cy),
            half(7 * ZC, 2 * cr), half(7 * ZC, 2 * cr), half(16, 2 * cy),
            pltpu.VMEM((4, nc, 7 * ZC, cy), F32), pltpu.VMEM((4, nc, 7 * ZC, cy), F32),
            pltpu.VMEM((4, nc, 16, cr), F32), pltpu.VMEM((4, nc, 16, cr), F32),
            pltpu.VMEM((devices, 8, 128), F32), pltpu.VMEM((devices, 8, 128), F32),
            pltpu.VMEM((STEPS, cx, cy), F32),
            dma((12,)), dma((max(nc, 3), 3)), dma((4, nc, 4)), dma((4, nc, 4)), dma((devices,)), dma((devices,)),
        ],
        compiler_params=pltpu.CompilerParams(
            collective_id=0, has_side_effects=True, vmem_limit_bytes=62 * 2**20),
        name="steps",
    )(flat(pressure), flat(velocity), flat(kappa), flat(buoyancy), flat(fwd_pressure),
      flat(gradient), traces, kernel, rec_tile.reshape(1, n_rows), rec_cell.reshape(1, n_rows))
    press, vel, grad = pl.pallas_call(
        functools.partial(hand_out, nc),
        out_shape=shapes,
        in_specs=[hbm] * 3,
        out_specs=(hbm,) * 3,
        scratch_shapes=[dma((nc, 5))],
        compiler_params=pltpu.CompilerParams(vmem_limit_bytes=62 * 2**20),
        name="hand_out",
    )(*results)
    return (press.reshape(nz, cx, cy), vel.reshape(3, nz, cx, cy), grad.reshape(nz, cx, cy))


def solution(mesh):
    return jax.shard_map(
        local,
        mesh=mesh,
        in_specs=(
            P(None, "tx", "ty"),
            P(None, None, "tx", "ty"),
            P(None, "tx", "ty"),
            P(None, None, "tx", "ty"),
            P(None, None, "tx", "ty"),
            P(None, "tx", "ty"),
            P(("tx", "ty"), None),
            P(),
            P(("tx", "ty"), None),
            P(("tx", "ty")),
        ),
        out_specs=(P(None, "tx", "ty"), P(None, None, "tx", "ty"), P(None, "tx", "ty")),
        check_vma=False,
    )
```

time: 86.7 us -> 264 us (3.04)
  Pallas kernels: 57.2 us -> 263 us
  blocking collectives: 14.3 us -> 0 us
  local copies, waits for them, and re-layouts: 13.3 us -> 0 us
    pallas_call x1, Pallas kernels: 1.45 us -> 200 us  [local(): pl.pallas_call(functools.partial(hand_out, nc), out_shape=shapes, in_spec...]
    all_to_all x1 -> x0, blocking collectives: 14.3 us -> none  [local(): lax.all_to_all(packed, ('tx', 'ty'), split_axis=1, concat_axis=1, tiled=T...]
    unnamed x27 -> x0, local copies, waits for them, and re-layouts: 12.7 us -> none
    pallas_call x1, Pallas kernels: 55.8 us -> 63.3 us  [local(): pl.pallas_call(functools.partial(step_kernel, n_tx, n_ty, nz, cx, cy), ou...]
where the time goes in v2:
time: 264 us
  Pallas kernels  263 us (100%)
    pallas_call x1, Pallas kernels, local(): pl.pallas_call(functools.partial(hand_out, nc), out_shape=shapes, in_spec...  200 us
    pallas_call x1, Pallas kernels, local(): pl.pallas_call(functools.partial(step_kernel, n_tx, n_ty, nz, cx, cy), ou...  63.3 us

profile of v2, /device:TPU:0, one launch (start us, length us, event | category | flops | bytes accessed | tf_op | source)
XLA Modules:
  0.0 263.8 jit_solution(17592302401594104083)
XLA Ops:
  0.6 63.3 %steps.1 = (f32[1280,256]{1,0:T(8,128)}, f32[3,1280,256]{2,1,0:T(8,128)}, f32[1280,256]{1,0:T(8,128)}) custom-call(f32[1280,256]{1,0:T(8,128)} %bitcast.14, f32[3,1280,256]{2,1,0:T(8,128)} %bitcast.11, f32[1280,256]{1,0:T(8,128)} %bitcast.15, f32[3,1280,256]{2,1,0:T(8,128)} %bitcast.12, f32[2,1280,256]{2,1,0:T(8,128)} %bitcast.13, f32[1280,256]{1,0:T(8,128)} %bitcast.16, ...), custom_call_target="tpu_custom_call" | custom-call | tf_op jit(solution)/shard_map/steps/pallas_call | solution.py:421
  64.0 199.9 %hand_out.1 = (f32[1280,256]{1,0:T(8,128)}, f32[3,1280,256]{2,1,0:T(8,128)}, f32[1280,256]{1,0:T(8,128)}) custom-call(f32[1280,256]{1,0:T(8,128)} %get-tuple-element.9.p_in, f32[3,1280,256]{2,1,0:T(8,128)} %get-tuple-element.10.v_in, f32[1280,256]{1,0:T(8,128)} %get-tuple-element.11.g_in), custom_call_target="tpu_custom_call" | custom-call | tf_op jit(solution)/shard_map/hand_out/pallas_call | solution.py:445

commit v3 on v2

--- a/solution.py
+++ b/solution.py
@@ -47,22 +47,27 @@
 FAR = 1 << 20
 
 
+def log2(n):
+    return n.bit_length() - 1
+
+
 def build_x(ref, cx, plus):
     cr = ZC * cx
     low = 3 if plus else 4
     row, col = grid_of((cr, cr))
-    hi, lo = taps(jnp.where(row // cx == col // cx, col % cx - row % cx, FAR), plus)
+    sx, mx = log2(cx), cx - 1
+    hi, lo = taps(jnp.where(row >> sx == col >> sx, (col & mx) - (row & mx), FAR), plus)
     ref[:, 0:cr] = hi.astype(BF16)
     ref[:, cr:2 * cr] = hi.astype(BF16)
     ref[:, 2 * cr:3 * cr] = lo.astype(BF16)
-    width = 7 * ZC
-    row, col = grid_of((cr, ref.shape[1] - 3 * cr))
-    seg = jnp.where(col < width, 0, jnp.where(col < 2 * width, 1, jnp.where(col < 3 * width, 2, 3)))
-    at = col - seg * width
-    layer = at // ZC
+    row, col = grid_of((cr, 128))
+    layer = col >> log2(ZC)
     x = jnp.where(layer < low, layer - low, cx + layer - low)
-    hi, lo = taps(jnp.where(row // cx == at % ZC, x - row % cx, FAR), plus)
-    ref[:, 3 * cr:] = jnp.where(seg < 2, hi, jnp.where(seg == 2, lo, 0.0)).astype(BF16)
+    near = (row >> sx == col & (ZC - 1)) & (layer < 7)
+    hi, lo = taps(jnp.where(near, x - (row & mx), FAR), plus)
+    ref[:, 3 * cr:3 * cr + 128] = hi.astype(BF16)
+    ref[:, 3 * cr + 128:3 * cr + 256] = hi.astype(BF16)
+    ref[:, 3 * cr + 256:] = lo.astype(BF16)
 
 
 def build_y(ref, cy, plus):
@@ -72,7 +77,7 @@
     ref[cy:2 * cy] = hi.astype(BF16)
     ref[2 * cy:3 * cy] = lo.astype(BF16)
     row, col = grid_of((ref.shape[0] - 3 * cy, cy))
-    seg, at = row // 16, row % 16
+    seg, at = row >> 4, row & 15
     hi, lo = taps(jnp.where(at < 8, at - 8, cy + at - 8) - col, plus)
     ref[3 * cy:] = jnp.where(seg < 2, hi, jnp.where(seg == 2, lo, 0.0)).astype(BF16)
 
@@ -80,15 +85,10 @@
 def build_x_edges(ref, cx, plus):
     low = 3 if plus else 4
     row, col = grid_of(ref.shape)
-    at = col % (ZC * cx)
-    layer = row // ZC
+    at = col & (ZC * cx - 1)
+    layer = row >> log2(ZC)
     x = jnp.where(layer < low, cx - low + layer, layer - low)
-    ref[...] = jnp.where(at == (row % ZC) * cx + x, 1.0, 0.0).astype(BF16)
-
-
-def build_y_edges(ref, cy):
-    row, col = grid_of(ref.shape)
-    ref[...] = jnp.where(col % cy == jnp.where(row < 8, cy - 8 + row, row - 8), 1.0, 0.0).astype(BF16)
+    ref[...] = jnp.where(at == (row & (ZC - 1)) * cx + x, 1.0, 0.0).astype(BF16)
 
 
 def split(v):
@@ -124,7 +124,7 @@
     packed = None
     for v in (hi, lo):
         spread = jnp.concatenate([v] * devices, axis=0)
-        to = lax.broadcasted_iota(jnp.int32, (devices * 8, rows), 0) // 8 == tiles
+        to = lax.broadcasted_iota(jnp.int32, (devices * 8, rows), 0) >> 3 == tiles
         part = dot_nt(jnp.where(to, spread, 0.0).astype(BF16), place)
         packed = part if packed is None else packed + part
     return packed.reshape(devices, 8, 128)
@@ -134,7 +134,7 @@
                 p_in, v_in, kap_in, b_in, fwd_in, g_in, traces_in, kernel_in, tile_in, cell_in,
                 p_out, v_out, g_out,
                 p, vx, vy, vz, kap, buo, fwd, grad, traces, filt, tiles, cells,
-                xp, xm, yp, ym, sxp, sxm, sy,
+                xp, xm, yp, ym, sxp, sxm,
                 xs, xr, ys, yr, ts, tr, inj,
                 in_sem, out_sem, send_sem, recv_sem, to_sem, from_sem):
     tx, ty = lax.axis_index("tx"), lax.axis_index("ty")
@@ -190,7 +190,6 @@
         clear(d)
 
     build_x_edges(sxp, cx, True)
-    build_y_edges(sy, cy)
     pl.semaphore_wait(barrier, devices - 1)
 
     def halo_copy(ph, c, d):
@@ -225,15 +224,16 @@
     def post(ph, c, pick, fx, fy):
         hi, lo = split(fx)
         xs[ph, c] = dot(pick[...], jnp.concatenate([hi, lo], axis=0))
-        hi, lo = split(fy)
-        ys[ph, c] = dot_nt(sy[...], jnp.concatenate([hi, lo], axis=1))
+        lane = lax.broadcasted_iota(jnp.int32, (cr, 128), 1)
+        turned = jnp.where(lane < 8, fy[:, 0:128], fy[:, cy - 128:cy]).T
+        ys[ph, c] = jnp.concatenate([turned[120:128], turned[0:8]], axis=0)
         send(ph, c)
 
     def x_diff(ph, c, field, matrix):
         hi, lo = split(field)
         hh, hl = split(xr[ph, c])
-        tail = jnp.zeros((48, cy), BF16)
-        return dot(matrix[...], jnp.concatenate([hi, lo, hi, hh, hl, hh, tail], axis=0))
+        gap = jnp.zeros((16, cy), BF16)
+        return dot(matrix[...], jnp.concatenate([hi, lo, hi, hh, gap, hl, gap, hh, gap], axis=0))
 
     def y_diff(ph, c, field, matrix):
         hi, lo = split(field)
@@ -385,18 +385,22 @@
         copy.wait()
 
 
-def hand_out(n_chunks, p_in, v_in, g_in, p_out, v_out, g_out, sem):
+def hand_out(n_chunks, p_in, v_in, g_in, p_out, v_out, g_out, held, sem_in, sem_out):
     rows = p_in.shape[0] // n_chunks
-    copies = []
+    reads, writes = [], []
     for c in range(n_chunks):
         at = pl.ds(c * rows, rows)
-        copies.append(pltpu.make_async_copy(p_in.at[at], p_out.at[at], sem.at[c, 0]))
-        copies.append(pltpu.make_async_copy(g_in.at[at], g_out.at[at], sem.at[c, 1]))
-        for i in range(3):
-            copies.append(pltpu.make_async_copy(v_in.at[i, at], v_out.at[i, at], sem.at[c, 2 + i]))
-    for copy in copies:
+        ends = [(p_in.at[at], p_out.at[at]), (g_in.at[at], g_out.at[at])]
+        ends += [(v_in.at[i, at], v_out.at[i, at]) for i in range(3)]
+        for i, (a, b) in enumerate(ends):
+            reads.append(pltpu.make_async_copy(a, held.at[i, at], sem_in.at[c, i]))
+            writes.append(pltpu.make_async_copy(held.at[i, at], b, sem_out.at[c, i]))
+    for copy in reads:
         copy.start()
-    for copy in copies:
+    for read, write in zip(reads, writes):
+        read.wait()
+        write.start()
+    for copy in writes:
         copy.wait()
 
 
@@ -430,7 +434,7 @@
             pltpu.VMEM((1, n_rows), jnp.int32), pltpu.VMEM((1, n_rows), jnp.int32),
             half(cr, 3 * cr + 384), half(cr, 3 * cr + 384),
             half(3 * cy + 128, cy), half(3 * cy + 128, cy),
-            half(7 * ZC, 2 * cr), half(7 * ZC, 2 * cr), half(16, 2 * cy),
+            half(7 * ZC, 2 * cr), half(7 * ZC, 2 * cr),
             pltpu.VMEM((4, nc, 7 * ZC, cy), F32), pltpu.VMEM((4, nc, 7 * ZC, cy), F32),
             pltpu.VMEM((4, nc, 16, cr), F32), pltpu.VMEM((4, nc, 16, cr), F32),
             pltpu.VMEM((devices, 8, 128), F32), pltpu.VMEM((devices, 8, 128), F32),
@@ -447,7 +451,7 @@
         out_shape=shapes,
         in_specs=[hbm] * 3,
         out_specs=(hbm,) * 3,
-        scratch_shapes=[dma((nc, 5))],
+        scratch_shapes=[field(5), dma((nc, 5)), dma((nc, 5))],
         compiler_params=pltpu.CompilerParams(vmem_limit_bytes=62 * 2**20),
         name="hand_out",
     )(*results)

time: 264 us -> 69.7 us (0.26)
  Pallas kernels: 263 us -> 68.9 us
    pallas_call x1, Pallas kernels: 200 us -> 5.66 us  [local(): pl.pallas_call(functools.partial(hand_out, nc), out_shape=shapes, in_spec...]
where the time goes in v3:
time: 69.7 us; the launch traced here: 69.6 us
  Pallas kernels  68.9 us (99%)
    pallas_call x1, Pallas kernels, local(): pl.pallas_call(functools.partial(step_kernel, n_tx, n_ty, nz, cx, cy), ou...  63.2 us
    pallas_call x1, Pallas kernels, local(): pl.pallas_call(functools.partial(hand_out, nc), out_shape=shapes, in_spec...  5.66 us

profile of v3, /device:TPU:0, one launch (start us, length us, event | category | flops | bytes accessed | tf_op | source)
XLA Modules:
  0.0 69.6 jit_solution(11804509119436581692)
XLA Ops:
  0.6 63.2 %steps.1 = (f32[1280,256]{1,0:T(8,128)}, f32[3,1280,256]{2,1,0:T(8,128)}, f32[1280,256]{1,0:T(8,128)}) custom-call(f32[1280,256]{1,0:T(8,128)} %bitcast.14, f32[3,1280,256]{2,1,0:T(8,128)} %bitcast.11, f32[1280,256]{1,0:T(8,128)} %bitcast.15, f32[3,1280,256]{2,1,0:T(8,128)} %bitcast.12, f32[2,1280,256]{2,1,0:T(8,128)} %bitcast.13, f32[1280,256]{1,0:T(8,128)} %bitcast.16, ...), custom_call_target="tpu_custom_call" | custom-call | tf_op jit(solution)/shard_map/steps/pallas_call | solution.py:425
  63.9 5.7 %hand_out.1 = (f32[1280,256]{1,0:T(8,128)}, f32[3,1280,256]{2,1,0:T(8,128)}, f32[1280,256]{1,0:T(8,128)}) custom-call(f32[1280,256]{1,0:T(8,128)} %get-tuple-element.9.p_in, f32[3,1280,256]{2,1,0:T(8,128)} %get-tuple-element.10.v_in, f32[1280,256]{1,0:T(8,128)} %get-tuple-element.11.g_in), custom_call_target="tpu_custom_call" | custom-call | tf_op jit(solution)/shard_map/hand_out/pallas_call | solution.py:449
